TPU v7x, 256 devices: a whole 4x4x8 slice. The times are simulated.
256 devices in a mesh: row: 8 (over x_hi, y), col: 32 (over x_lo, z, core).
Axes of the slice: x: 4 (x_hi: 2, x_lo: 2; x = x_hi * 2 + x_lo), y: 4, z: 8, core: 2. Of those that a mesh axis runs over, the one named last changes fastest.
Arguments:
- features: bfloat16 [65536, 256], P(('col', 'row')), may hold values from -6 to 6
- edge_tiles: bfloat16 [8, 6144, 128, 128], P('row', 'col'), may hold values from 0 to 0.020874023
- tile_slot: int32 [8, 6144], P('row', 'col'), may hold values from 0 to 1023, as said below
- tile_count: int32 [8, 32], P('row', 'col'), may hold values from 24 to 192, as said below
- weight: bfloat16 [256, 256], replicated, may hold values from -0.375 to 0.375
- cotangent: bfloat16 [65536, 256], P(('row', 'col')), may hold values from -6 to 6
Outputs:
- layer_out: bfloat16 [65536, 256], P(('row', 'col'))
- weight_grad: float32 [256, 256], replicated
- feature_grad: bfloat16 [65536, 256], P(('col', 'row'))
Inputs may be any that keep to these rules, and one draw needn't show every extreme that they name: `tile_slot`: the positions of the 192 slots of one device are distinct cells of its block's tile grid, numbered row by row. `tile_count`: some device has all 192 slots live.
All inputs are finite; a program needn't handle non-finite values.
Results may differ from a plain program's by a relative error of at most 0.0061.
Values may be sent and summed in bfloat16 or wider, within the bound.
A program may use at most 128 MiB of HBM per device.

v0:
```python
import math

import jax
import jax.numpy as jnp
from jax import lax
from jax.sharding import PartitionSpec as P


def add_forward(row_accum, tile_group, pos_group, valid_mask, x_panel3, col_tiles):
    row_index = pos_group // col_tiles
    col_index = pos_group % col_tiles
    x_tiles = jnp.take(x_panel3, col_index, axis=0)
    product = jnp.einsum("gab,gbh->gah", tile_group, x_tiles, preferred_element_type=jnp.float32)
    product = product * valid_mask.astype(jnp.float32)[:, None, None]
    return row_accum.at[row_index].add(product)


def add_backward(col_accum, tile_group, pos_group, valid_mask, grad_rows3, col_tiles):
    row_index = pos_group // col_tiles
    col_index = pos_group % col_tiles
    y_tiles = jnp.take(grad_rows3, row_index, axis=0)
    product = jnp.einsum("gab,gah->gbh", tile_group, y_tiles, preferred_element_type=jnp.float32)
    product = product * valid_mask.astype(jnp.float32)[:, None, None]
    return col_accum.at[col_index].add(product)


def sweep(
    accum,
    adder,
    tile_stack,
    pos_stack,
    first_valid,
    end_valid,
    group_size,
    context,
    col_tiles,
    group_total,
):

    def visit(group_index, running):
        start = group_index * group_size
        tile_group = lax.dynamic_slice_in_dim(tile_stack, start, group_size, 0)
        pos_group = lax.dynamic_slice_in_dim(pos_stack, start, group_size, 0)
        slot_ids = start + jnp.arange(group_size, dtype=jnp.int32)
        valid_mask = (slot_ids >= first_valid) & (slot_ids < end_valid)
        return adder(running, tile_group, pos_group, valid_mask, context, col_tiles)

    return lax.fori_loop(0, group_total, visit, accum)


def body(features, edge_tiles, tile_slot, tile_count, weight, cotangent):
    n_row = lax.axis_size("row")
    n_col = lax.axis_size("col")
    node_dev, hidden_width = features.shape
    tile_size = edge_tiles.shape[-1]
    slot_total = edge_tiles.shape[1]
    tile_stack = edge_tiles.reshape(slot_total, tile_size, tile_size)
    slot_pos = tile_slot.reshape(slot_total)
    live_count = tile_count.reshape(())
    row_tiles = node_dev * n_col // tile_size
    col_tiles = node_dev * n_row // tile_size
    lend_slots = slot_total // 4
    group_size = math.gcd(16, lend_slots)
    x_panel = lax.all_gather(features, "row", axis=0, tiled=True)
    x_panel3 = x_panel.reshape(col_tiles, tile_size, hidden_width)
    own_groups = (live_count + group_size - 1) // group_size
    row_accum = jnp.zeros((row_tiles, tile_size, hidden_width), jnp.float32)
    row_accum = sweep(
        row_accum,
        add_forward,
        tile_stack,
        slot_pos,
        0,
        live_count,
        group_size,
        x_panel3,
        col_tiles,
        own_groups,
    )
    aggregated = lax.psum_scatter(
        row_accum.reshape(row_tiles * tile_size, hidden_width),
        "col",
        scatter_dimension=0,
        tiled=True,
    )
    hidden = aggregated.astype(jnp.bfloat16)
    preact = jnp.dot(hidden, weight, preferred_element_type=jnp.float32)
    sigma_pre = jax.nn.sigmoid(preact)
    layer_out = (preact * sigma_pre).astype(jnp.bfloat16)
    act_grad = (
        cotangent.astype(jnp.float32) * sigma_pre * (1.0 + preact * (1.0 - sigma_pre))
    ).astype(jnp.bfloat16)
    weight_part = jnp.einsum("nk,nh->kh", hidden, act_grad, preferred_element_type=jnp.float32)
    node_total = node_dev * n_row * n_col
    weight_grad = lax.psum(weight_part, ("row", "col")) * float(node_total) ** (-0.5)
    hidden_grad = jnp.dot(act_grad, weight.T, preferred_element_type=jnp.float32).astype(
        jnp.bfloat16
    )
    grad_rows = lax.all_gather(hidden_grad, "col", axis=0, tiled=True)
    grad_rows3 = grad_rows.reshape(row_tiles, tile_size, hidden_width)
    col_accum = jnp.zeros((col_tiles, tile_size, hidden_width), jnp.float32)
    col_accum = sweep(
        col_accum,
        add_backward,
        tile_stack,
        slot_pos,
        0,
        live_count,
        group_size,
        grad_rows3,
        col_tiles,
        own_groups,
    )
    feature_sum = lax.psum_scatter(
        col_accum.reshape(col_tiles * tile_size, hidden_width),
        "row",
        scatter_dimension=0,
        tiled=True,
    )
    feature_grad = feature_sum.astype(jnp.bfloat16)
    return (layer_out, weight_grad, feature_grad)


def solution(mesh):
    in_specs = (
        P(("col", "row"), None),
        P("row", "col", None, None),
        P("row", "col"),
        P("row", "col"),
        P(),
        P(("row", "col"), None),
    )
    out_specs = (P(("row", "col"), None), P(), P(("col", "row"), None))
    return jax.shard_map(body, mesh=mesh, in_specs=in_specs, out_specs=out_specs, check_vma=False)
```

profile of v0, /device:TPU:1, one launch (start us, length us, event | category | flops | bytes accessed | tf_op | source)
XLA Modules:
  0.0 714.1 jit_solution(12387883481262118541)
XLA Ops:
  8.6 55.8 %all-gather.3.cloned.1.call-done = bf16[2048,256]{1,0:T(8,128)(2,1)} async-done(((bf16[256,256]{1,0:T(8,128)(2,1)}), bf16[2048,256]{1,0:T(8,128)(2,1)}) %all-gather.3.cloned.1.call-update) | async-done | bytes 1048592 | tf_op jit(solution)/shard_map/all_gather | solution.py:64
  64.5 4.3 broadcast_in_dim.62
  68.7 52.6 %while.24 = (s32[]{:T(128)}, f32[64,128,256]{2,1,0:T(8,128)}, s32[]{:T(128)}, s32[192]{0:T(256)S(1)}, bf16[192,128,128]{2,1,0:T(8,128)(2,1)}, /*index=5*/bf16[16...) while((s32[]{:T(128)}, f32[64,128,256]{2,1,0:T(8,128)}, ...), condition=%wide.region_2.3_spmd, body=%wide.region_0.2_spmd.sunk | while | flops 135792208 | bytes 12063631 | solution.py:48
  69.5 1.8 gather_fusion
  71.3 1.5 convolution_multiply_fusion.4
  73.0 4.5 scatter_fusion
  78.2 1.8 gather_fusion
  80.1 1.5 convolution_multiply_fusion.4
  81.7 4.5 scatter_fusion
  86.9 1.8 gather_fusion
  88.8 1.5 convolution_multiply_fusion.4
  90.4 4.6 scatter_fusion
  95.8 1.8 gather_fusion
  97.6 1.5 convolution_multiply_fusion.4
  99.2 4.6 scatter_fusion
  104.6 1.8 gather_fusion
  106.4 1.5 convolution_multiply_fusion.4
  108.1 4.5 scatter_fusion
  113.3 1.8 gather_fusion
  116.8 4.6 scatter_fusion
  121.4 177.7 %reduce-scatter.3.cloned.1.call-done = f32[256,256]{1,0:T(8,128)} async-done(((f32[8192,256]{1,0:T(8,128)}), f32[256,256]{1,0:T(8,128)}) %reduce-scatter.3.cloned.1.call-update) | async-done | bytes 262160 | tf_op jit(solution)/shard_map/reduce_scatter | solution.py:80
  299.2 1.9 multiply_convert_fusion
  302.1 8.7 %copy.9 = bf16[1,192,128,128]{2,3,1,0:T(8,128)(2,1)} copy(bf16[1,192,128,128]{3,2,1,0:T(8,128)(2,1)} %bitcast.16) | data formatting | bytes 12582912 | tf_op args[1]
  311.7 57.5 %all-gather.5.cloned.1.call-done = bf16[8192,256]{1,0:T(8,128)(2,1)} async-done(((bf16[256,256]{1,0:T(8,128)(2,1)}), bf16[8192,256]{1,0:T(8,128)(2,1)}) %all-gather.5.cloned.1.call-update) | async-done | bytes 4194320 | tf_op jit(solution)/shard_map/all_gather | solution.py:99
  369.2 1.6 broadcast_in_dim.63
  370.7 57.0 %while.25 = (s32[]{:T(128)}, f32[16,128,256]{2,1,0:T(8,128)}, s32[]{:T(128)}, s32[192]{0:T(256)S(1)}, bf16[192,128,128]{1,2,0:T(8,128)(2,1)}, /*index=5*/bf16[64...) while((s32[]{:T(128)}, f32[16,128,256]{2,1,0:T(8,128)}, ...), condition=%wide.region_7.8_spmd, body=%wide.region_5.7_spmd.sunk | while | flops 135792160 | bytes 12063563 | solution.py:48
  371.5 2.8 gather_fusion.1
  374.3 1.5 convolution_multiply_fusion.5
  375.9 4.4 scatter_fusion.1
  381.0 2.8 gather_fusion.1
  383.8 1.5 convolution_multiply_fusion.5
  385.4 4.4 scatter_fusion.1
  390.5 2.8 gather_fusion.1
  393.3 1.5 convolution_multiply_fusion.5
  394.9 4.3 scatter_fusion.1
  399.9 2.8 gather_fusion.1
  402.8 1.5 convolution_multiply_fusion.5
  404.3 4.4 scatter_fusion.1
  409.5 2.8 gather_fusion.1
  412.3 1.5 convolution_multiply_fusion.5
  413.9 4.5 scatter_fusion.1
  419.1 2.8 gather_fusion.1
  421.9 1.5 convolution_multiply_fusion.5
  423.5 4.3 scatter_fusion.1
  427.8 195.6 %all-reduce.2.cloned.1.call-done = f32[256,256]{1,0:T(8,128)} async-done(((f32[256,256]{1,0:T(8,128)}), f32[256,256]{1,0:T(8,128)}) %all-reduce.2.cloned.1.call-update) | async-done | bytes 262160 | tf_op jit(solution)/shard_map/psum | solution.py:95
  623.4 1.7 broadcast_multiply_fusion
  625.1 80.9 %reduce-scatter.5.cloned.1.call-done = f32[256,256]{1,0:T(8,128)} async-done(((f32[2048,256]{1,0:T(8,128)}), f32[256,256]{1,0:T(8,128)}) %reduce-scatter.5.cloned.1.call-update) | async-done | bytes 262160 | tf_op jit(solution)/shard_map/reduce_scatter | solution.py:114
  706.0 1.6 convert_element_type.43
  (57 shorter events, 13.7 us)
Async XLA Ops:
  7.2 292.0 %copy-start = (bf16[256,256]{1,0:T(8,128)(2,1)S(1)}, bf16[256,256]{1,0:T(8,128)(2,1)}, u32[]{:S(2)}) copy-start(bf16[256,256]{1,0:T(8,128)(2,1)} %param.14) | copy-start | bytes 393220
  7.2 57.3 %all-gather.3.cloned.1.call-start = ((), (), s32[]{:S(2)}) async-start(), calls=%async_computation.2 | async-start | bytes 1179648 | tf_op jit(solution)/shard_map/all_gather | solution.py:64
  7.9 291.3 %reduce-scatter.3.cloned.1.call-start = ((), (), s32[]{:S(2)}) async-start(), calls=%async_computation.3 | async-start | bytes 8650752 | tf_op jit(solution)/shard_map/reduce_scatter | solution.py:80
  64.5 4.3 copy-start.2
  121.4 177.8 %copy-start.3 = (bf16[256,256]{1,0:T(8,128)(2,1)S(1)}, bf16[256,256]{1,0:T(8,128)(2,1)}, u32[]{:S(2)}) copy-start(bf16[256,256]{1,0:T(8,128)(2,1)} %param.15) | copy-start | bytes 393220
  121.4 247.8 %all-gather.5.cloned.1.call-start = ((), (), s32[]{:S(2)}) async-start(), calls=%async_computation.5 | async-start | bytes 4325376 | tf_op jit(solution)/shard_map/all_gather | solution.py:99
  302.0 8.7 %copy-start.1 = (f32[256,256]{1,0:T(8,128)S(1)}, f32[256,256]{1,0:T(8,128)}, u32[]{:S(2)}) copy-start(f32[256,256]{1,0:T(8,128)} %reduce-scatter.3.cloned.1.call-done) | copy-start | bytes 786436
  302.0 321.4 %all-reduce.2.cloned.1.call-start = ((), (), s32[]{:S(2)}) async-start(), calls=%async_computation.4 | async-start | bytes 524288 | tf_op jit(solution)/shard_map/psum | solution.py:95
  311.7 394.3 %reduce-scatter.5.cloned.1.call-start = ((), (), s32[]{:S(2)}) async-start(), calls=%async_computation.6 | async-start | bytes 2359296 | tf_op jit(solution)/shard_map/reduce_scatter | solution.py:114
Sparse Core Ops, SparseCore 0:
  10.7 53.7 all-gather.2
  121.5 177.6 reduce-scatter.2
  302.1 67.0 all-gather.4
  375.1 248.2 all-reduce.1
  627.2 78.6 reduce-scatter.4
where the time goes:
time: 718 us; the launch traced here: 714 us
  waiting for transfers between devices  568 us (79%)
  other arithmetic  66.2 us (9%)
  local copies, waits for them, and re-layouts  42.4 us (6%)
  matrix products  22.2 us (3%)
  between operations  14.5 us (2%)
    psum x1, waiting for transfers between devices, body(): lax.psum(weight_part, ('row', 'col')) * float(node_total) ** (-0.5)  196 us
    reduce_scatter x1, waiting for transfers between devices, body(): lax.psum_scatter(row_accum.reshape(row_tiles * tile_size, hidden_width),...  178 us
    reduce_scatter x1, waiting for transfers between devices, body(): lax.psum_scatter(col_accum.reshape(col_tiles * tile_size, hidden_width),...  80.9 us
    all_gather x1, waiting for transfers between devices, body(): grad_rows = lax.all_gather(hidden_grad, 'col', axis=0, tiled=True)  57.5 us
    all_gather x1, waiting for transfers between devices, body(): x_panel = lax.all_gather(features, 'row', axis=0, tiled=True)  55.8 us
    scatter-add x6, other arithmetic, add_forward(): return row_accum.at[row_index].add(product)  27.3 us
    scatter-add x6, other arithmetic, add_backward(): return col_accum.at[col_index].add(product)  26.2 us
    gather x6, local copies, waits for them, and re-layouts, add_backward(): y_tiles = jnp.take(grad_rows3, row_index, axis=0)  16.9 us
  transfers between devices with their start and end apart: 5, of which 5 were waited for; matrix products, arithmetic and copies ran while one was open for 10% of the time, Pallas kernels for 0%

commit v1 on v0

v1 whole, which is shorter than its diff:
```python
import functools

import jax
import jax.numpy as jnp
from jax import lax
from jax.experimental import pallas as pl
from jax.experimental.pallas import tpu as pltpu
from jax.sharding import PartitionSpec as P

F32 = jnp.float32
BF16 = jnp.bfloat16
MESH = pl.DeviceIdType.MESH
N = 256
A = 128
B = 128
DIST = (4, 3, -3, 2, -2, 1, -1, 0)
SEMS = dict(
    feat=8, core=8, xrow=8, ringz=16, ringx=8, xfin=1,
    own=8, part=8, xv=1, xu=8, pair=8,
    w1=8, w2=8, w3=4, w4=8, w5=8, grad=8,
)
OFFSET = {}
TOTAL = 0
for _name, _count in SEMS.items():
    OFFSET[_name] = TOTAL
    TOTAL += _count


def kernel(
    inv, feat, tiles_hbm, weight, cot,
    layer_out, weight_grad, feature_grad,
    tiles, xpan, pf, ks, kr, sxs, sx, rx, zs, rz, qs, rq, xfs, xfr, zf,
    hp, acc, w1s, w1r, w2s, w2r, w3r, w4r, w5r, gs, gr,
    ssem, rsem, tsem,
):
    r = lax.axis_index("row")
    c = lax.axis_index("col")
    xh, y = r // 4, r % 4
    xl, z, k = c // 16, (c % 16) // 2, c % 2
    ox, ok = 1 - xl, 1 - k

    def row_of(i):
        return ((xh + i // 4) % 2) * 4 + (y + i % 4) % 4

    def row_from(i):
        return ((xh + i // 4) % 2) * 4 + (y + 4 - i % 4) % 4

    def at_row(i):
        return (row_of(i), c)

    def at_z(d):
        return (r, xl * 16 + ((z + d + 8) % 8) * 2 + k)

    def at_x():
        return (r, ox * 16 + z * 2 + k)

    def at_core():
        return (r, xl * 16 + z * 2 + ok)

    def at_mate(i):
        return (r, ((xl + i // 2) % 2) * 16 + z * 2 + (k + i % 2) % 2)

    sent = []

    def desc(src, dst, name, i, to):
        return pltpu.make_async_remote_copy(
            src_ref=src, dst_ref=dst, send_sem=ssem.at[OFFSET[name] + i],
            recv_sem=rsem.at[OFFSET[name] + i], device_id=to, device_id_type=MESH,
        )

    def send(src, dst, name, i, to):
        d = desc(src, dst, name, i, to)
        d.start()
        sent.append(d)

    def arrive(dst, name, i):
        desc(dst, dst, name, i, at_core()).wait_recv()

    load = pltpu.make_async_copy(tiles_hbm, tiles.at[pl.ds(0, 192)], tsem)
    load.start()
    barrier = pltpu.get_barrier_semaphore()
    for i in range(1, 8):
        pl.semaphore_signal(barrier, inc=1, device_id=at_row(i), device_id_type=MESH)
        pl.semaphore_signal(barrier, inc=1, device_id=at_z(i), device_id_type=MESH)
    for i in range(1, 4):
        pl.semaphore_signal(barrier, inc=1, device_id=at_mate(i), device_id_type=MESH)
    tiles[192] = jnp.zeros((128, 128), BF16)
    xpan[r] = feat[...]
    pl.semaphore_wait(barrier, 17)

    for i in (4, 1, 3, 2, 5, 7, 6):
        send(feat, xpan.at[r], "feat", i, at_row(i))
    load.wait()
    for i in (4, 1, 3, 2, 5, 7, 6):
        arrive(xpan.at[row_from(i)], "feat", i)

    def forward(g):
        zt = (z + DIST[g] + 8) % 8

        @pl.loop(0, 2)
        def _(h):
            kt = ok + h * (2 * k - 1)
            total = None
            for p in range(8):
                rows = []
                for q in range(4):
                    cell = (2 * ((q // 2) * 16 + zt * 2 + kt) + q % 2) * 16 + 2 * p
                    rows.append(jnp.concatenate([tiles[inv[cell]], tiles[inv[cell + 1]]], axis=1))
                part = jnp.dot(jnp.concatenate(rows, axis=0), xpan[p], preferred_element_type=F32)
                total = part if total is None else total + part
            pf[g % 2, h] = total

        for q in range(2):
            ks[g, q] = pf[g % 2, 0, pl.ds(q * N, N)].astype(BF16)
        send(ks.at[g], kr.at[g], "core", g, at_core())

    def way(d):
        return (0, 4 - d) if d > 0 else (1, 4 + d)

    def process_z(g):
        d, par = DIST[g], g % 2
        arrive(kr.at[g], "core", g)
        sxs[g] = (pf[par, 1, pl.ds(ox * N, A)] + kr[g, ox, 0:A].astype(F32)).astype(BF16)
        send(sxs.at[g], rx.at[g], "xrow", g, at_x())
        if d != 0:
            for q in range(2):
                s = pf[par, 1, pl.ds(q * N + A, N - A)] + kr[g, q, A:N].astype(F32)
                if d == 4:
                    w, step = q, 0
                else:
                    w, step = way(d)
                    if step > 1 or q == w:
                        arrive(rz.at[w, step - 1, q], "ringz", (w * 4 + step - 1) * 2 + q)
                        s = s + rz[w, step - 1, q].astype(F32)
                zs[g, q] = s.astype(BF16)
                send(zs.at[g, q], rz.at[w, step, q], "ringz", (w * 4 + step) * 2 + q, at_z(1 - 2 * w))
        sx[g] = pf[par, 1, pl.ds(xl * N, A)] + kr[g, xl, 0:A].astype(F32)

    def process_x(g):
        d = DIST[g]
        arrive(rx.at[g], "xrow", g)
        s = sx[g] + rx[g].astype(F32)
        if d == 4:
            qs[g] = s.astype(BF16)
            for w in range(2):
                rows = pl.ds(w * (A // 2), A // 2)
                send(qs.at[g, rows], rq.at[w, 0, rows], "ringx", w * 4, at_z(1 - 2 * w))
            return
        w, step = way(d)
        if step == 1:
            rows = pl.ds(w * (A // 2), A // 2)
            arrive(rq.at[w, 0, rows], "ringx", w * 4)
            sx[g] = s
            sx[g, rows] += rq[w, 0, rows].astype(F32)
            s = sx[g]
        else:
            arrive(rq.at[w, step - 1], "ringx", w * 4 + step - 1)
            s = s + rq[w, step - 1].astype(F32)
        qs[g] = s.astype(BF16)
        send(qs.at[g], rq.at[w, step], "ringx", w * 4 + step, at_z(1 - 2 * w))

    forward(0)
    process_z(0)
    forward(1)
    forward(2)
    process_z(1)
    process_z(2)
    process_x(0)
    forward(3)
    process_x(1)
    process_x(2)
    forward(4)
    process_z(3)
    process_z(4)
    forward(5)
    process_x(3)
    process_x(4)
    forward(6)
    process_z(5)
    process_z(6)
    forward(7)
    process_x(5)
    process_x(6)
    process_z(7)
    for w in range(2):
        for q in range(2):
            arrive(rz.at[w, 3, q], "ringz", (w * 4 + 3) * 2 + q)
    xfs[...] = (
        pf[1, 1, pl.ds(ox * N + A, N - A)] + kr[7, ox, A:N].astype(F32)
        + rz[0, 3, ox].astype(F32) + rz[1, 3, ox].astype(F32)
    ).astype(BF16)
    send(xfs, xfr, "xfin", 0, at_x())
    zf[...] = (
        pf[1, 1, pl.ds(xl * N + A, N - A)] + kr[7, xl, A:N].astype(F32)
        + rz[0, 3, xl].astype(F32) + rz[1, 3, xl].astype(F32)
    )
    arrive(rx.at[7], "xrow", 7)
    for w in range(2):
        arrive(rq.at[w, 3], "ringx", w * 4 + 3)
    head = (sx[7] + rx[7].astype(F32) + rq[0, 3].astype(F32) + rq[1, 3].astype(F32)).astype(BF16)
    arrive(xfr, "xfin", 0)
    tail = (zf[...] + xfr[...].astype(F32)).astype(BF16)

    hidden = jnp.concatenate([head, tail], axis=0)
    preact = jnp.dot(hidden, weight[...], preferred_element_type=F32)
    sig = jax.nn.sigmoid(preact)
    layer_out[...] = (preact * sig).astype(BF16)
    act = (cot[...].astype(F32) * sig * (1.0 + preact * (1.0 - sig))).astype(BF16)
    hp[z, k, xl] = jnp.dot(act, weight[...].T, preferred_element_type=F32).astype(BF16)

    head_rows, tail_rows = pl.ds(0, B), pl.ds(B, N - B)
    mine = hp.at[z, k, xl]
    send(mine.at[tail_rows], mine.at[tail_rows], "xv", 0, at_x())
    send(mine, mine, "own", 0, at_z(1))
    send(mine, mine, "own", 4, at_z(-1))
    send(mine.at[head_rows], mine.at[head_rows], "xu", 0, at_x())

    w1s[...] = jnp.dot(hidden.T, act, preferred_element_type=F32).reshape(8, 32, N)
    for i in range(1, 8):
        send(w1s.at[row_of(i)], w1r.at[r], "w1", i, at_row(i))
    acc[...] = jnp.zeros_like(acc)

    def place(d):
        return (z + d + 8) % 8

    def came_from(w, step):
        return place(-1 - step) if w == 0 else place(1 + step)

    def number(d):
        return d if d >= 0 else 8 + d

    def own_step(w, step):
        to = at_z(1 - 2 * w)
        dist = -1 - step if w == 0 else 1 + step
        block = hp.at[came_from(w, step), k, xl]
        if step < 3:
            arrive(block, "own", w * 4 + step)
            if step < 2:
                send(block, block, "own", w * 4 + step + 1, to)
            else:
                half = block.at[pl.ds(w * 128, 128)]
                send(half, half, "own", w * 4 + 3, to)
            send(block.at[head_rows], block.at[head_rows], "xu", number(dist), at_x())
        else:
            half = block.at[pl.ds(w * 128, 128)]
            arrive(half, "own", w * 4 + 3)
            if w == 0:
                send(half, half, "xu", 4, at_x())

    def part_step(w, step):
        to = at_z(1 - 2 * w)
        block = hp.at[came_from(w, step), k, ox]
        rows = block.at[tail_rows] if step < 3 else block.at[pl.ds(B + w * 64, 64)]
        arrive(rows, "part", w * 4 + step)
        if step < 2:
            send(rows, rows, "part", w * 4 + step + 1, to)
        elif step == 2:
            half = block.at[pl.ds(B + w * 64, 64)]
            send(half, half, "part", w * 4 + 3, to)

    def share(d):
        block = hp.at[place(d), k, ox, head_rows]
        arrive(block, "xu", number(d))
        both = hp.at[place(d), k]
        send(both, both, "pair", number(d), at_core())

    def have(d):
        arrive(hp.at[place(d), ok], "pair", number(d))

    def backward(d, first, last):
        zt = place(d)
        left = jnp.concatenate([hp[zt, q // 2, q % 2] for q in range(4)], axis=0).T

        @pl.loop(first, last)
        def _(n):
            acc[n] += jnp.dot(left, right_of(zt, n), preferred_element_type=F32)

    def right_of(zt, n):
        rows = []
        for q in range(8):
            block = ((q // 2) % 2) * 16 + zt * 2 + q // 4
            cell = (2 * block + q % 2) * 16 + 2 * n
            rows.append(jnp.concatenate([tiles[inv[cell]], tiles[inv[cell + 1]]], axis=1))
        return jnp.concatenate(rows, axis=0)

    arrive(hp.at[z, k, ox, tail_rows], "xv", 0)
    block = hp.at[z, k, ox, tail_rows]
    send(block, block, "part", 0, at_z(1))
    send(block, block, "part", 4, at_z(-1))
    share(0)
    own_step(0, 0)
    own_step(1, 0)
    have(0)
    backward(0, 0, 4)
    part_step(0, 0)
    part_step(1, 0)
    backward(0, 4, 8)
    for i in range(1, 8):
        arrive(w1r.at[row_from(i)], "w1", i)
    w1r[r] = w1s[r]
    s = w1r[0]
    for i in range(1, 8):
        s = s + w1r[i]
    for i in range(8):
        w2s[i] = s[(i // 2) * 8:(i // 2) * 8 + 8, (i % 2) * 128:(i % 2) * 128 + 128]
    for i in range(1, 8):
        send(w2s.at[place(i)], w2r.at[z], "w2", i, at_z(i))
    share(-1)
    share(1)
    own_step(0, 1)
    own_step(1, 1)
    have(-1)
    backward(-1, 0, 4)
    part_step(0, 1)
    part_step(1, 1)
    backward(-1, 4, 8)
    have(1)
    backward(1, 0, 8)
    for i in range(1, 8):
        arrive(w2r.at[place(-i)], "w2", i)
    w2r[z] = w2s[z]
    s = w2r[0]
    for i in range(1, 8):
        s = s + w2r[i]
    w3r[xl * 2 + k] = s
    for i in range(1, 4):
        send(w3r.at[xl * 2 + k], w3r.at[xl * 2 + k], "w3", i, at_mate(i))
    share(-2)
    own_step(0, 2)
    own_step(1, 2)
    share(2)
    have(-2)
    backward(-2, 0, 4)
    part_step(0, 2)
    part_step(1, 2)
    backward(-2, 4, 8)
    for i in range(1, 4):
        arrive(w3r.at[((xl + i // 2) % 2) * 2 + (k + i % 2) % 2], "w3", i)
    w4r[z] = (w3r[0] + w3r[1]) + (w3r[2] + w3r[3])
    for i in range(1, 8):
        send(w4r.at[z], w4r.at[z], "w4", i, at_z(i))
    have(2)
    backward(2, 0, 4)
    own_step(0, 3)
    backward(2, 4, 8)
    share(-3)
    share(3)
    have(-3)
    backward(-3, 0, 8)
    own_step(1, 3)
    part_step(0, 3)
    part_step(1, 3)
    share(4)
    for i in range(1, 8):
        arrive(w4r.at[place(-i)], "w4", i)
    for i in range(8):
        w5r[r, (i // 2) * 8:(i // 2) * 8 + 8, (i % 2) * 128:(i % 2) * 128 + 128] = w4r[i]
    for i in range(1, 8):
        send(w5r.at[r], w5r.at[r], "w5", i, at_row(i))
    have(3)
    backward(3, 0, 8)
    have(4)

    zt = place(4)
    left = jnp.concatenate([hp[zt, q // 2, q % 2] for q in range(4)], axis=0).T

    @pl.loop(0, 8)
    def _(j):
        i = (j + 1) % 8
        n = row_of(i)
        acc[n] += jnp.dot(left, right_of(zt, n), preferred_element_type=F32)

        @pl.when(i != 0)
        def _():
            gs[n] = acc[n].astype(BF16)
            desc(gs.at[n], gr.at[r], "grad", i, at_row(i)).start()

    for i in range(1, 8):
        arrive(w5r.at[row_from(i)], "w5", i)
    weight_grad[...] = w5r[...].reshape(N, N) * (65536.0 ** -0.5)
    s = acc[r]
    for i in range(1, 8):
        arrive(gr.at[row_from(i)], "grad", i)
        s = s + gr[row_from(i)].astype(F32)
    feature_grad[...] = s.T.astype(BF16)
    for d in sent:
        d.wait_send()
    for i in range(1, 8):
        desc(gs.at[row_of(i)], gr.at[r], "grad", i, at_row(i)).wait_send()


def body(features, edge_tiles, tile_slot, tile_count, weight, cotangent):
    slots = tile_slot.reshape(192)
    ids = jnp.arange(192, dtype=jnp.int32)
    slots = jnp.where(ids < tile_count.reshape(()), slots, -1)
    cells = jnp.arange(1024, dtype=jnp.int32)
    hit = slots[None, :] == cells[:, None]
    inv = 192 + jnp.sum(jnp.where(hit, ids[None, :] - 192, 0), axis=1, dtype=jnp.int32)
    vmem = pl.BlockSpec(memory_space=pltpu.VMEM)

    def buf(*shape, dtype=BF16):
        return pltpu.VMEM(shape, dtype)

    return pl.pallas_call(
        kernel,
        out_shape=(
            jax.ShapeDtypeStruct((N, N), BF16),
            jax.ShapeDtypeStruct((N, N), F32),
            jax.ShapeDtypeStruct((N, N), BF16),
        ),
        in_specs=[pl.BlockSpec(memory_space=pltpu.SMEM), vmem, pl.BlockSpec(memory_space=pl.ANY), vmem, vmem],
        out_specs=(vmem, vmem, vmem),
        scratch_shapes=[
            buf(193, 128, 128),
            buf(8, N, N),
            buf(2, 2, 2 * N, N, dtype=F32),
            buf(8, 2, N, N),
            buf(8, 2, N, N),
            buf(8, A, N),
            buf(8, A, N, dtype=F32),
            buf(8, A, N),
            buf(7, 2, N - A, N),
            buf(2, 4, 2, N - A, N),
            buf(7, A, N),
            buf(2, 4, A, N),
            buf(N - A, N),
            buf(N - A, N),
            buf(N - A, N, dtype=F32),
            buf(8, 2, 2, N, N),
            buf(8, N, N, dtype=F32),
            buf(8, 32, N, dtype=F32),
            buf(8, 32, N, dtype=F32),
            buf(8, 8, 128, dtype=F32),
            buf(8, 8, 128, dtype=F32),
            buf(4, 8, 128, dtype=F32),
            buf(8, 8, 128, dtype=F32),
            buf(8, 32, N, dtype=F32),
            buf(8, N, N),
            buf(8, N, N),
            pltpu.SemaphoreType.DMA((TOTAL,)),
            pltpu.SemaphoreType.DMA((TOTAL,)),
            pltpu.SemaphoreType.DMA,
        ],
        compiler_params=pltpu.CompilerParams(
            collective_id=0, has_side_effects=True, vmem_limit_bytes=56 * 2**20
        ),
    )(inv, features, edge_tiles.reshape(192, 128, 128), weight, cotangent)


def solution(mesh):
    in_specs = (
        P(("col", "row"), None),
        P("row", "col", None, None),
        P("row", "col"),
        P("row", "col"),
        P(),
        P(("row", "col"), None),
    )
    out_specs = (P(("row", "col"), None), P(), P(("col", "row"), None))
    return jax.shard_map(body, mesh=mesh, in_specs=in_specs, out_specs=out_specs, check_vma=False)
```

time: 718 us -> 114 us (0.16)
  waiting for transfers between devices: 568 us -> 0 us
  Pallas kernels: 0 us -> 106 us
  other arithmetic: 66.2 us -> 1.44 us
  local copies, waits for them, and re-layouts: 42.4 us -> 4.8 us
  matrix products: 22.2 us -> 0 us
  between operations: 14.5 us -> 1.29 us
    reduce_scatter x2 -> x0, waiting for transfers between devices: 259 us -> none  [the longest x1 178 us: body(): lax.psum_scatter(row_accum.reshape(row_tiles * tile_size, hidden_width),...]
    psum x1 -> x0, waiting for transfers between devices: 196 us -> none  [body(): lax.psum(weight_part, ('row', 'col')) * float(node_total) ** (-0.5)]
    all_gather x2 -> x0, waiting for transfers between devices: 113 us -> none  [the longest x1 57.5 us: body(): grad_rows = lax.all_gather(hidden_grad, 'col', axis=0, tiled=True)]
    pallas_call x0 -> x1, Pallas kernels: none -> 106 us  [body(): pl.pallas_call(kernel, out_shape=(jax.ShapeDtypeStruct((N, N), BF16), jax...]
    scatter-add x12 -> x0, other arithmetic: 53.5 us -> none  [the longest x6 27.3 us: add_forward(): return row_accum.at[row_index].add(product)]
    gather x12 -> x0, local copies, waits for them, and re-layouts: 27.9 us -> none  [the longest x6 16.9 us: add_backward(): y_tiles = jnp.take(grad_rows3, row_index, axis=0)]
    dot_general x15 -> x0, matrix products: 22.2 us -> none  [the longest x6 9.28 us: add_backward(): jnp.einsum('gab,gah->gbh', tile_group, y_tiles, preferred_element_type=jn...]
    and x12 -> x0, other arithmetic: 8.79 us -> none  [the longest x6 4.39 us: add_backward(): y_tiles = jnp.take(grad_rows3, row_index, axis=0)]
  transfers between devices with their start and end apart: 5 -> 0, of which waited for: 5 -> 0; matrix products, arithmetic and copies ran while one was open for 10% -> 0% of each run, Pallas kernels for 0% -> 0%
where the time goes in v1:
time: 114 us; the launch traced here: 113 us
  Pallas kernels  106 us (93%)
  local copies, waits for them, and re-layouts  4.8 us (4%)
  other arithmetic  1.44 us (1%)
  between operations  1.29 us (1%)
    pallas_call x1, Pallas kernels, body(): pl.pallas_call(kernel, out_shape=(jax.ShapeDtypeStruct((N, N), BF16), jax...  106 us
    unnamed x3, local copies, waits for them, and re-layouts  4.8 us

profile of v1, /device:TPU:1, one launch (start us, length us, event | category | flops | bytes accessed | tf_op | source)
XLA Modules:
  0.0 113.4 jit_solution(13652702788816310919)
XLA Ops:
  1.3 0.7 compare_select_fusion
  2.0 0.2 select_reduce_fusion
  2.1 0.6 broadcast_add_fusion.inv
  2.7 105.8 %shard_map.85 = (bf16[256,256]{1,0:T(8,128)(2,1)}, f32[256,256]{1,0:T(8,128)}, bf16[256,256]{1,0:T(8,128)(2,1)}) custom-call(s32[1024]{0:T(1024)} %broadcast_add_fusion.inv, bf16[256,256]{1,0:T(8,128)(2,1)} %feat.1, bf16[192,128,128]{2,1,0:T(8,128)(2,1)} %bitcast.4, bf16[256,256]{1,0:T(8,128)(2,1)} %weight.1, bf16[256,256]{1,0:T(8,128)(2,1)} %cot.1), custom_call_target="tpu_custom_call" | custom-call | tf_op jit(solution)/shard_map/pallas_call | solution.py:404
  108.5 1.6 %copy.13 = bf16[256,256]{1,0:T(8,128)(2,1)} copy(bf16[256,256]{1,0:T(8,128)(2,1)} %get-tuple-element.6) | data formatting | bytes 262144
  110.1 1.7 %copy.14 = f32[256,256]{1,0:T(8,128)} copy(f32[256,256]{1,0:T(8,128)} %get-tuple-element.7) | data formatting | bytes 524288
  111.8 1.6 %copy.15 = bf16[256,256]{1,0:T(8,128)(2,1)} copy(bf16[256,256]{1,0:T(8,128)(2,1)} %get-tuple-element.8) | data formatting | bytes 262144
  (1 shorter events, 0.0 us)

commit v2 on v1

v2 whole, which is shorter than its diff:
```python
import functools

import jax
import jax.numpy as jnp
from jax import lax
from jax.experimental import pallas as pl
from jax.experimental.pallas import tpu as pltpu
from jax.sharding import PartitionSpec as P

F32 = jnp.float32
BF16 = jnp.bfloat16
MESH = pl.DeviceIdType.MESH
N = 256
A = 128
B = 128
DIST = (4, 3, -3, 2, -2, 1, -1, 0)
SEMS = dict(
    feat=8, core=8, xrow=8, ringz=16, ringx=8, xfin=1,
    head=8, tail=8, part=8, xv=1, xu=8, pair=8,
    w1=8, w2=8, w3=4, w4=8, w5=8, grad=8,
)
SUMS = (
    "Fa0", "Fb0", "Fa1", "Fb1", "S0", "Z00", "Z01", "Fa2", "S1", "Z11", "Fb2", "Fa3", "S2", "Z20", "Fb3", "X0", "Z10",
    "Z21", "S3", "Fa4", "Fb4", "Z31", "Fa5", "S4", "Z40", "X1", "Fb5", "X2", "S5", "Z30", "Fa6", "Z41", "Fb6", "Z51",
    "Fa7", "S6", "Z60", "X3", "Fb7", "X4", "S7", "Z50", "Z61", "X5", "X6", "P0", "P1", "P2", "P3",
)
GATHER = (
    "W1", "OH00", "OH10", "V", "SH0", "OT10", "OT00", "C0,0", "OH01", "OH11", "C0,1", "C0,2", "C0,3", "PT10", "PT00",
    "SH-1", "W2", "OT01", "OT11", "SH1", "C-1,0", "C-1,1", "OH12", "OH02", "C-1,2", "C-1,3", "PT01", "SH-2", "PT11",
    "SH2", "C1,0", "C1,1", "OT02", "OT12", "C1,2", "W3", "C1,3", "OH03", "C-2,0", "C-2,1", "PT12", "PT02", "SH3",
    "SH-3", "C-2,2", "C-2,3", "OT13", "W4", "C2,0", "C2,1", "C2,2", "PT13", "PT03", "SH4", "C2,3", "C-3,0", "C-3,1",
    "C-3,2", "C-3,3", "C3,0", "W5", "C3,1", "C3,2", "C3,3",
)
OFFSET = {}
TOTAL = 0
for _name, _count in SEMS.items():
    OFFSET[_name] = TOTAL
    TOTAL += _count


def kernel(
    slots, count, feat, tiles_hbm, weight_hbm, cot_hbm,
    layer_out, weight_grad, feature_grad,
    tiles, xpan, pacc, ks, kr, sxs, sx, rx, zs, rz, qs, rq, xfs, xfr, zf,
    hp, lt, acc, w1s, w1r, w2s, w2r, w3r, w4r, w5r, gs, gr, weight, cot, inv_v, inv,
    ssem, rsem, tsem,
):
    r = lax.axis_index("row")
    c = lax.axis_index("col")
    xh, y = r // 4, r % 4
    xl, z, k = c // 16, (c % 16) // 2, c % 2
    ox, ok = 1 - xl, 1 - k

    def row_of(i):
        return ((xh + i // 4) % 2) * 4 + (y + i % 4) % 4

    def row_from(i):
        return ((xh + i // 4) % 2) * 4 + (y + 4 - i % 4) % 4

    def at_row(i):
        return (row_of(i), c)

    def at_z(d):
        return (r, xl * 16 + ((z + d + 8) % 8) * 2 + k)

    def at_x():
        return (r, ox * 16 + z * 2 + k)

    def at_core():
        return (r, xl * 16 + z * 2 + ok)

    def at_mate(i):
        return (r, ((xl + i // 2) % 2) * 16 + z * 2 + (k + i % 2) % 2)

    sent = []

    def desc(src, dst, name, i, to):
        return pltpu.make_async_remote_copy(
            src_ref=src, dst_ref=dst, send_sem=ssem.at[OFFSET[name] + i],
            recv_sem=rsem.at[OFFSET[name] + i], device_id=to, device_id_type=MESH,
        )

    def send(src, dst, name, i, to):
        d = desc(src, dst, name, i, to)
        d.start()
        sent.append(d)

    def arrive(dst, name, i):
        desc(dst, dst, name, i, at_core()).wait_recv()

    barrier = pltpu.get_barrier_semaphore()
    for i in range(1, 8):
        pl.semaphore_signal(barrier, inc=1, device_id=at_row(i), device_id_type=MESH)
        pl.semaphore_signal(barrier, inc=1, device_id=at_z(i), device_id_type=MESH)
    for i in range(1, 4):
        pl.semaphore_signal(barrier, inc=1, device_id=at_mate(i), device_id_type=MESH)
    local = [
        pltpu.make_async_copy(src, dst, tsem.at[i])
        for i, (src, dst) in enumerate((
            (feat, xpan.at[r]), (tiles_hbm, tiles.at[pl.ds(0, 192)]), (weight_hbm, weight), (cot_hbm, cot),
        ))
    ]
    for copy in local:
        copy.start()
    tiles[192] = jnp.zeros((128, 128), BF16)
    cell = lax.broadcasted_iota(jnp.int32, (8, 128), 0) * 128 + lax.broadcasted_iota(jnp.int32, (8, 128), 1)
    live = count[0, 0]

    def find(s, table):
        return jnp.where((cell == slots[0, s]) & (s < live), s, table)

    inv_v[...] = lax.fori_loop(0, 192, find, jnp.full((8, 128), 192, jnp.int32), unroll=8)
    place_table = pltpu.make_async_copy(inv_v, inv, tsem.at[4])
    place_table.start()
    local[0].wait()
    pl.semaphore_wait(barrier, 17)

    for i in (4, 1, 3, 2, 5, 7, 6):
        send(xpan.at[r], xpan.at[r], "feat", i, at_row(i))
    place_table.wait()
    local[1].wait()

    def pair(row, p):
        n, at = row // 8, (row % 8) * 16 + 2 * p
        return jnp.concatenate([tiles[inv[n, at]], tiles[inv[n, at + 1]]], axis=1)

    def product(zt, kt, blocks):
        total = None
        for p in blocks:
            rows = [pair(2 * ((q // 2) * 16 + zt * 2 + kt) + q % 2, p) for q in range(4)]
            part = jnp.dot(jnp.concatenate(rows, axis=0), xpan[p], preferred_element_type=F32)
            total = part if total is None else total + part
        return total

    @pl.loop(0, 16)
    def _(j):
        pacc[j // 2, j % 2] = product(j // 2, j % 2, [r])

    for i in (1, 3, 4):
        arrive(xpan.at[row_from(i)], "feat", i)

    @pl.loop(0, 16)
    def _(j):
        pacc[j // 2, j % 2] += product(j // 2, j % 2, [row_from(i) for i in (1, 3, 4)])

    for i in (2, 5, 7, 6):
        arrive(xpan.at[row_from(i)], "feat", i)

    def side(q):
        return xl if q else ox

    def forward(g, h):
        zt = (z + DIST[g] + 8) % 8
        kt = k if h else ok
        pacc[zt, kt] += product(zt, kt, [row_from(i) for i in (2, 5, 7, 6)])
        if h == 0:
            for q in range(2):
                ks[g, q] = pacc[zt, kt, pl.ds(q * N, N)].astype(BF16)
            send(ks.at[g], kr.at[g], "core", g, at_core())

    def chip_sum(g, q, first, last):
        zt, x = (z + DIST[g] + 8) % 8, side(q)
        return pacc[zt, k, pl.ds(x * N + first, last - first)] + kr[g, x, first:last].astype(F32)

    def way(d):
        return (0, 4 - d) if d > 0 else (1, 4 + d)

    def chip(g):
        arrive(kr.at[g], "core", g)
        sxs[g] = chip_sum(g, 0, 0, A).astype(BF16)
        send(sxs.at[g], rx.at[g], "xrow", g, at_x())
        sx[g] = chip_sum(g, 1, 0, A)

    def ring_z(g, q):
        s = chip_sum(g, q, A, N)
        w, step = (q, 0) if DIST[g] == 4 else way(DIST[g])
        if step > 1 or (step == 1 and q == w):
            arrive(rz.at[w, step - 1, q], "ringz", (w * 4 + step - 1) * 2 + q)
            s = s + rz[w, step - 1, q].astype(F32)
        zs[g, q] = s.astype(BF16)
        send(zs.at[g, q], rz.at[w, step, q], "ringz", (w * 4 + step) * 2 + q, at_z(1 - 2 * w))

    def ring_x(g):
        d = DIST[g]
        arrive(rx.at[g], "xrow", g)
        s = sx[g] + rx[g].astype(F32)
        if d == 4:
            qs[g] = s.astype(BF16)
            for w in range(2):
                rows = pl.ds(w * (A // 2), A // 2)
                send(qs.at[g, rows], rq.at[w, 0, rows], "ringx", w * 4, at_z(1 - 2 * w))
            return
        w, step = way(d)
        if step == 1:
            rows = pl.ds(w * (A // 2), A // 2)
            arrive(rq.at[w, 0, rows], "ringx", w * 4)
            sx[g] = s
            sx[g, rows] += rq[w, 0, rows].astype(F32)
            s = sx[g]
        else:
            arrive(rq.at[w, step - 1], "ringx", w * 4 + step - 1)
            s = s + rq[w, step - 1].astype(F32)
        qs[g] = s.astype(BF16)
        send(qs.at[g], rq.at[w, step], "ringx", w * 4 + step, at_z(1 - 2 * w))

    def last_z(q):
        for w in range(2):
            arrive(rz.at[w, 3, q], "ringz", (w * 4 + 3) * 2 + q)
        s = chip_sum(7, q, A, N) + rz[0, 3, q].astype(F32) + rz[1, 3, q].astype(F32)
        if q == 0:
            xfs[...] = s.astype(BF16)
            send(xfs, xfr, "xfin", 0, at_x())
        else:
            zf[...] = s

    for op in SUMS:
        if op[:2] == "Fa":
            forward(int(op[2]), 0)
        elif op[:2] == "Fb":
            forward(int(op[2]), 1)
        elif op[0] == "S":
            chip(int(op[1]))
        elif op[0] == "Z":
            ring_z(int(op[1]), int(op[2]))
        elif op[0] == "X":
            ring_x(int(op[1]))
        elif op in ("P0", "P1"):
            last_z(int(op[1]))
    arrive(rx.at[7], "xrow", 7)
    for w in range(2):
        arrive(rq.at[w, 3], "ringx", w * 4 + 3)
    head = (sx[7] + rx[7].astype(F32) + rq[0, 3].astype(F32) + rq[1, 3].astype(F32)).astype(BF16)
    arrive(xfr, "xfin", 0)
    tail = (zf[...] + xfr[...].astype(F32)).astype(BF16)
    local[2].wait()
    local[3].wait()

    hidden = jnp.concatenate([head, tail], axis=0)
    preact = jnp.dot(hidden, weight[...], preferred_element_type=F32)
    sig = jax.nn.sigmoid(preact)
    layer_out[...] = (preact * sig).astype(BF16)
    act = (cot[...].astype(F32) * sig * (1.0 + preact * (1.0 - sig))).astype(BF16)
    hp[z, k, xl] = jnp.dot(act, weight[...].T, preferred_element_type=F32).astype(BF16)

    head_rows, tail_rows = pl.ds(0, B), pl.ds(B, N - B)
    mine = hp.at[z, k, xl]
    mine_head, mine_tail = mine.at[head_rows], mine.at[tail_rows]
    send(mine_tail, mine_tail, "xv", 0, at_x())
    send(mine_head, mine_head, "head", 0, at_z(1))
    send(mine_head, mine_head, "head", 4, at_z(-1))
    send(mine_head, mine_head, "xu", 0, at_x())
    send(mine_tail, mine_tail, "tail", 0, at_z(1))
    send(mine_tail, mine_tail, "tail", 4, at_z(-1))

    def place(d):
        return (z + d + 8) % 8

    def came_from(w, step):
        return place(-1 - step) if w == 0 else place(1 + step)

    def number(d):
        return d if d >= 0 else 8 + d

    def head_step(w, step):
        dist = 4 if step == 3 else (1 + step if w else -1 - step)
        rows = hp.at[came_from(w, step), k, xl, head_rows]
        arrive(rows, "head", w * 4 + step)
        if step < 2 or (step == 2 and w == 0):
            send(rows, rows, "head", w * 4 + step + 1, at_z(1 - 2 * w))
        send(rows, rows, "xu", number(dist), at_x())

    def tail_step(w, step):
        rows = hp.at[came_from(w, step), k, xl, tail_rows]
        arrive(rows, "tail", w * 4 + step)
        if step < 2 or (step == 2 and w == 1):
            send(rows, rows, "tail", w * 4 + step + 1, at_z(1 - 2 * w))

    def part_step(w, step):
        to = at_z(1 - 2 * w)
        block = hp.at[came_from(w, step), k, ox]
        rows = block.at[tail_rows] if step < 3 else block.at[pl.ds(B + w * 64, 64)]
        arrive(rows, "part", w * 4 + step)
        if step < 2:
            send(rows, rows, "part", w * 4 + step + 1, to)
        elif step == 2:
            half = block.at[pl.ds(B + w * 64, 64)]
            send(half, half, "part", w * 4 + 3, to)

    def share(d):
        block = hp.at[place(d), k, ox, head_rows]
        arrive(block, "xu", number(d))
        both = hp.at[place(d), k]
        send(both, both, "pair", number(d), at_core())

    def have(d):
        arrive(hp.at[place(d), ok], "pair", number(d))
        lt[...] = jnp.concatenate([hp[place(d), q // 2, q % 2] for q in range(4)], axis=0).T

    def add_product(d, n):
        rows = [pair(2 * (((q // 2) % 2) * 16 + place(d) * 2 + q // 4) + q % 2, n) for q in range(8)]
        acc[n] += jnp.dot(lt[...], jnp.concatenate(rows, axis=0), preferred_element_type=F32)

    def backward(d, part):
        if part == 0:
            have(d)

        @pl.loop(2 * part, 2 * part + 2)
        def _(n):
            add_product(d, n)

    def x_tail():
        rows = hp.at[z, k, ox, tail_rows]
        arrive(rows, "xv", 0)
        send(rows, rows, "part", 0, at_z(1))
        send(rows, rows, "part", 4, at_z(-1))

    def gradient_step(step):
        if step == 1:
            w1s[...] = jnp.dot(hidden.T, act, preferred_element_type=F32).reshape(8, 32, N)
            for i in range(1, 8):
                send(w1s.at[row_of(i)], w1r.at[r], "w1", i, at_row(i))
            acc[...] = jnp.zeros_like(acc)
        elif step == 2:
            for i in range(1, 8):
                arrive(w1r.at[row_from(i)], "w1", i)
            w1r[r] = w1s[r]
            s = w1r[0]
            for i in range(1, 8):
                s = s + w1r[i]
            for i in range(8):
                w2s[i] = s[(i // 2) * 8:(i // 2) * 8 + 8, (i % 2) * 128:(i % 2) * 128 + 128]
            for i in range(1, 8):
                send(w2s.at[place(i)], w2r.at[z], "w2", i, at_z(i))
        elif step == 3:
            for i in range(1, 8):
                arrive(w2r.at[place(-i)], "w2", i)
            w2r[z] = w2s[z]
            s = w2r[0]
            for i in range(1, 8):
                s = s + w2r[i]
            w3r[xl * 2 + k] = s
            for i in range(1, 4):
                send(w3r.at[xl * 2 + k], w3r.at[xl * 2 + k], "w3", i, at_mate(i))
        elif step == 4:
            for i in range(1, 4):
                arrive(w3r.at[((xl + i // 2) % 2) * 2 + (k + i % 2) % 2], "w3", i)
            w4r[z] = (w3r[0] + w3r[1]) + (w3r[2] + w3r[3])
            for i in range(1, 8):
                send(w4r.at[z], w4r.at[z], "w4", i, at_z(i))
        else:
            for i in range(1, 8):
                arrive(w4r.at[place(-i)], "w4", i)
            for i in range(8):
                w5r[r, (i // 2) * 8:(i // 2) * 8 + 8, (i % 2) * 128:(i % 2) * 128 + 128] = w4r[i]
            for i in range(1, 8):
                send(w5r.at[r], w5r.at[r], "w5", i, at_row(i))

    for op in GATHER:
        if op[:2] == "OH":
            head_step(int(op[2]), int(op[3]))
        elif op[:2] == "OT":
            tail_step(int(op[2]), int(op[3]))
        elif op[:2] == "PT":
            part_step(int(op[2]), int(op[3]))
        elif op[:2] == "SH":
            share(int(op[2:]))
        elif op[0] == "C":
            d, part = op[1:].split(",")
            backward(int(d), int(part))
        elif op[0] == "W":
            gradient_step(int(op[1]))
        else:
            x_tail()

    have(4)

    @pl.loop(0, 8)
    def _(j):
        i = (j + 1) % 8
        n = row_of(i)
        add_product(4, n)

        @pl.when(i != 0)
        def _():
            gs[n] = acc[n].astype(BF16)
            desc(gs.at[n], gr.at[r], "grad", i, at_row(i)).start()

    for i in range(1, 8):
        arrive(w5r.at[row_from(i)], "w5", i)
    weight_grad[...] = w5r[...].reshape(N, N) * (65536.0 ** -0.5)
    s = acc[r]
    for i in range(1, 8):
        arrive(gr.at[row_from(i)], "grad", i)
        s = s + gr[row_from(i)].astype(F32)
    feature_grad[...] = s.T.astype(BF16)
    for d in sent:
        d.wait_send()
    for i in range(1, 8):
        desc(gs.at[row_of(i)], gr.at[r], "grad", i, at_row(i)).wait_send()


def hand_over(a, b, c, a_out, b_out, c_out):
    a_out[...] = a[...]
    b_out[...] = b[...]
    c_out[...] = c[...]


def body(features, edge_tiles, tile_slot, tile_count, weight, cotangent):
    vmem = pl.BlockSpec(memory_space=pltpu.VMEM)

    def buf(*shape, dtype=BF16):
        return pltpu.VMEM(shape, dtype)

    hbm = pl.BlockSpec(memory_space=pl.ANY)
    smem = pl.BlockSpec(memory_space=pltpu.SMEM)
    shapes = (
        jax.ShapeDtypeStruct((N, N), BF16),
        jax.ShapeDtypeStruct((N, N), F32),
        jax.ShapeDtypeStruct((N, N), BF16),
    )
    results = pl.pallas_call(
        kernel,
        out_shape=shapes,
        in_specs=[smem, smem, hbm, hbm, hbm, hbm],
        out_specs=(vmem, vmem, vmem),
        scratch_shapes=[
            buf(193, 128, 128),
            buf(8, N, N),
            buf(8, 2, 2 * N, N, dtype=F32),
            buf(8, 2, N, N),
            buf(8, 2, N, N),
            buf(8, A, N),
            buf(8, A, N, dtype=F32),
            buf(8, A, N),
            buf(7, 2, N - A, N),
            buf(2, 4, 2, N - A, N),
            buf(7, A, N),
            buf(2, 4, A, N),
            buf(N - A, N),
            buf(N - A, N),
            buf(N - A, N, dtype=F32),
            buf(8, 2, 2, N, N),
            buf(N, 4 * N),
            buf(8, N, N, dtype=F32),
            buf(8, 32, N, dtype=F32),
            buf(8, 32, N, dtype=F32),
            buf(8, 8, 128, dtype=F32),
            buf(8, 8, 128, dtype=F32),
            buf(4, 8, 128, dtype=F32),
            buf(8, 8, 128, dtype=F32),
            buf(8, 32, N, dtype=F32),
            buf(8, N, N),
            buf(8, N, N),
            buf(N, N),
            buf(N, N),
            buf(8, 128, dtype=jnp.int32),
            pltpu.SMEM((8, 128), jnp.int32),
            pltpu.SemaphoreType.DMA((TOTAL,)),
            pltpu.SemaphoreType.DMA((TOTAL,)),
            pltpu.SemaphoreType.DMA((5,)),
        ],
        compiler_params=pltpu.CompilerParams(
            collective_id=0, has_side_effects=True, vmem_limit_bytes=56 * 2**20
        ),
    )(tile_slot, tile_count, features, edge_tiles.reshape(192, 128, 128), weight, cotangent)
    return pl.pallas_call(
        hand_over,
        out_shape=shapes,
        in_specs=[vmem] * 3,
        out_specs=(vmem,) * 3,
    )(*results)


def solution(mesh):
    in_specs = (
        P(("col", "row"), None),
        P("row", "col", None, None),
        P("row", "col"),
        P("row", "col"),
        P(),
        P(("row", "col"), None),
    )
    out_specs = (P(("row", "col"), None), P(), P(("col", "row"), None))
    return jax.shard_map(body, mesh=mesh, in_specs=in_specs, out_specs=out_specs, check_vma=False)
```

time: 114 us -> 101 us (0.89)
  Pallas kernels: 106 us -> 98.5 us
  local copies, waits for them, and re-layouts: 4.8 us -> 0 us
  other arithmetic: 1.44 us -> 0 us
    pallas_call x1 -> x2, Pallas kernels: 106 us -> 98.5 us  [the longest x1 96.6 us: body(): pl.pallas_call(kernel, out_shape=shapes, in_specs=[smem, smem, hbm, hbm,...]
    unnamed x3 -> x0, local copies, waits for them, and re-layouts: 4.8 us -> none
where the time goes in v2:
time: 101 us; the launch traced here: 99.8 us
  Pallas kernels  98.5 us (98%)
  between operations  1.29 us (1%)
    pallas_call x1, Pallas kernels, body(): pl.pallas_call(kernel, out_shape=shapes, in_specs=[smem, smem, hbm, hbm,...  96.6 us

profile of v2, /device:TPU:1, one launch (start us, length us, event | category | flops | bytes accessed | tf_op | source)
XLA Modules:
  0.0 99.8 jit_solution(15551084569794736230)
XLA Ops:
  1.3 96.6 %shard_map.85 = (bf16[256,256]{1,0:T(8,128)(2,1)}, f32[256,256]{1,0:T(8,128)}, bf16[256,256]{1,0:T(8,128)(2,1)}) custom-call(s32[1,192]{1,0:T(1,128)} %slots.1, s32[1,1]{1,0:T(1,128)S(6)} %copy.9.count, bf16[256,256]{1,0:T(8,128)(2,1)} %feat.1, bf16[192,128,128]{2,1,0:T(8,128)(2,1)} %bitcast.1, bf16[256,256]{1,0:T(8,128)(2,1)} %weight_hbm.1, ...), custom_call_target="tpu_custom_call" | custom-call | tf_op jit(solution)/shard_map/pallas_call | solution.py:421
  97.9 1.8 %shard_map.86 = (bf16[256,256]{1,0:T(8,128)(2,1)}, f32[256,256]{1,0:T(8,128)}, bf16[256,256]{1,0:T(8,128)(2,1)}) custom-call(bf16[256,256]{1,0:T(8,128)(2,1)} %get-tuple-element.6.a, f32[256,256]{1,0:T(8,128)} %get-tuple-element.7.b, bf16[256,256]{1,0:T(8,128)(2,1)} %get-tuple-element.8.c), custom_call_target="tpu_custom_call" | custom-call | tf_op jit(solution)/shard_map/pallas_call | solution.py:466

commit v3 on v2

--- a/solution.py
+++ b/solution.py
@@ -25,11 +25,11 @@
     "Fa7", "S6", "Z60", "X3", "Fb7", "X4", "S7", "Z50", "Z61", "X5", "X6", "P0", "P1", "P2", "P3",
 )
 GATHER = (
-    "W1", "OH00", "OH10", "V", "SH0", "OT10", "OT00", "C0,0", "OH01", "OH11", "C0,1", "C0,2", "C0,3", "PT10", "PT00",
-    "SH-1", "W2", "OT01", "OT11", "SH1", "C-1,0", "C-1,1", "OH12", "OH02", "C-1,2", "C-1,3", "PT01", "SH-2", "PT11",
-    "SH2", "C1,0", "C1,1", "OT02", "OT12", "C1,2", "W3", "C1,3", "OH03", "C-2,0", "C-2,1", "PT12", "PT02", "SH3",
-    "SH-3", "C-2,2", "C-2,3", "OT13", "W4", "C2,0", "C2,1", "C2,2", "PT13", "PT03", "SH4", "C2,3", "C-3,0", "C-3,1",
-    "C-3,2", "C-3,3", "C3,0", "W5", "C3,1", "C3,2", "C3,3",
+    "OH00", "OH10", "V", "W1", "SH0", "OT10", "OT00", "C0,0", "OH01", "OH11", "C0,1", "C0,2", "C0,3", "PT10", "PT00",
+    "SH-1", "OT01", "OT11", "SH1", "C-1,0", "C-1,1", "OH12", "OH02", "W2", "C-1,2", "C-1,3", "PT01", "SH-2", "PT11",
+    "SH2", "C1,0", "C1,1", "OT02", "OT12", "C1,2", "C1,3", "OH03", "C-2,0", "C-2,1", "PT12", "PT02", "SH3", "SH-3",
+    "C-2,2", "C-2,3", "OT13", "C2,0", "C2,1", "C2,2", "PT13", "PT03", "SH4", "C2,3", "C-3,0", "C-3,1", "C-3,2",
+    "C-3,3", "W3", "C3,0", "C3,1", "C3,2", "C3,3", "W4",
 )
 OFFSET = {}
 TOTAL = 0
@@ -344,16 +344,15 @@
         elif step == 4:
             for i in range(1, 4):
                 arrive(w3r.at[((xl + i // 2) % 2) * 2 + (k + i % 2) % 2], "w3", i)
-            w4r[z] = (w3r[0] + w3r[1]) + (w3r[2] + w3r[3])
-            for i in range(1, 8):
-                send(w4r.at[z], w4r.at[z], "w4", i, at_z(i))
+            w4r[r] = (w3r[0] + w3r[1]) + (w3r[2] + w3r[3])
+            for i in range(1, 8):
+                send(w4r.at[r], w4r.at[r], "w4", i, at_row(i))
         else:
             for i in range(1, 8):
-                arrive(w4r.at[place(-i)], "w4", i)
-            for i in range(8):
-                w5r[r, (i // 2) * 8:(i // 2) * 8 + 8, (i % 2) * 128:(i % 2) * 128 + 128] = w4r[i]
-            for i in range(1, 8):
-                send(w5r.at[r], w5r.at[r], "w5", i, at_row(i))
+                arrive(w4r.at[row_from(i)], "w4", i)
+            w5r[z] = w4r[...]
+            for i in range(1, 8):
+                send(w5r.at[z], w5r.at[z], "w5", i, at_z(i))
 
     for op in GATHER:
         if op[:2] == "OH":
@@ -385,14 +384,18 @@
             gs[n] = acc[n].astype(BF16)
             desc(gs.at[n], gr.at[r], "grad", i, at_row(i)).start()
 
-    for i in range(1, 8):
-        arrive(w5r.at[row_from(i)], "w5", i)
-    weight_grad[...] = w5r[...].reshape(N, N) * (65536.0 ** -0.5)
+    gradient_step(5)
     s = acc[r]
     for i in range(1, 8):
         arrive(gr.at[row_from(i)], "grad", i)
         s = s + gr[row_from(i)].astype(F32)
     feature_grad[...] = s.T.astype(BF16)
+    for i in range(1, 8):
+        arrive(w5r.at[place(-i)], "w5", i)
+    for i in range(8):
+        for j in range(8):
+            first = j * 32 + (i // 2) * 8
+            weight_grad[first:first + 8, (i % 2) * 128:(i % 2) * 128 + 128] = w5r[i, j] * (65536.0 ** -0.5)
     for d in sent:
         d.wait_send()
     for i in range(1, 8):
@@ -448,7 +451,7 @@
             buf(8, 8, 128, dtype=F32),
             buf(4, 8, 128, dtype=F32),
             buf(8, 8, 128, dtype=F32),
-            buf(8, 32, N, dtype=F32),
+            buf(8, 8, 8, 128, dtype=F32),
             buf(8, N, N),
             buf(8, N, N),
             buf(N, N),

time: 101 us -> 101 us (level)
  no operation moved by 1% of the time
where the time goes in v3:
time: 101 us
  Pallas kernels  99.3 us (98%)
  between operations  1.29 us (1%)
    pallas_call x1, Pallas kernels, body(): pl.pallas_call(kernel, out_shape=shapes, in_specs=[smem, smem, hbm, hbm,...  97.5 us

profile of v3, /device:TPU:1, one launch (start us, length us, event | category | flops | bytes accessed | tf_op | source)
XLA Modules:
  0.0 100.6 jit_solution(10253187266418347785)
XLA Ops:
  1.3 97.5 %shard_map.85 = (bf16[256,256]{1,0:T(8,128)(2,1)}, f32[256,256]{1,0:T(8,128)}, bf16[256,256]{1,0:T(8,128)(2,1)}) custom-call(s32[1,192]{1,0:T(1,128)} %slots.1, s32[1,1]{1,0:T(1,128)S(6)} %copy.9.count, bf16[256,256]{1,0:T(8,128)(2,1)} %feat.1, bf16[192,128,128]{2,1,0:T(8,128)(2,1)} %bitcast.1, bf16[256,256]{1,0:T(8,128)(2,1)} %weight_hbm.1, ...), custom_call_target="tpu_custom_call" | custom-call | tf_op jit(solution)/shard_map/pallas_call | solution.py:424
  98.8 1.8 %shard_map.86 = (bf16[256,256]{1,0:T(8,128)(2,1)}, f32[256,256]{1,0:T(8,128)}, bf16[256,256]{1,0:T(8,128)(2,1)}) custom-call(bf16[256,256]{1,0:T(8,128)(2,1)} %get-tuple-element.6.a, f32[256,256]{1,0:T(8,128)} %get-tuple-element.7.b, bf16[256,256]{1,0:T(8,128)(2,1)} %get-tuple-element.8.c), custom_call_target="tpu_custom_call" | custom-call | tf_op jit(solution)/shard_map/pallas_call | solution.py:469

commit v4 on v3

--- a/solution.py
+++ b/solution.py
@@ -25,11 +25,11 @@
     "Fa7", "S6", "Z60", "X3", "Fb7", "X4", "S7", "Z50", "Z61", "X5", "X6", "P0", "P1", "P2", "P3",
 )
 GATHER = (
-    "OH00", "OH10", "V", "W1", "SH0", "OT10", "OT00", "C0,0", "OH01", "OH11", "C0,1", "C0,2", "C0,3", "PT10", "PT00",
-    "SH-1", "OT01", "OT11", "SH1", "C-1,0", "C-1,1", "OH12", "OH02", "W2", "C-1,2", "C-1,3", "PT01", "SH-2", "PT11",
-    "SH2", "C1,0", "C1,1", "OT02", "OT12", "C1,2", "C1,3", "OH03", "C-2,0", "C-2,1", "PT12", "PT02", "SH3", "SH-3",
-    "C-2,2", "C-2,3", "OT13", "C2,0", "C2,1", "C2,2", "PT13", "PT03", "SH4", "C2,3", "C-3,0", "C-3,1", "C-3,2",
-    "C-3,3", "W3", "C3,0", "C3,1", "C3,2", "C3,3", "W4",
+    "B0", "OH00", "OH10", "V", "W1", "OT10", "OT00", "SH0", "B1", "B-1", "C0,0", "C0,1", "OH01", "OH11", "C0,2",
+    "C0,3", "PT00", "SH-1", "PT10", "SH1", "OT01", "OT11", "C-1,0", "C-1,1", "C-1,2", "C-1,3", "OH12", "OH02", "C1,0",
+    "C1,1", "W2", "PT01", "PT11", "SH-2", "C1,2", "C1,3", "SH2", "OT02", "OT12", "C-2,0", "C-2,1", "OH03", "C-2,2",
+    "C-2,3", "C2,0", "PT02", "SH-3", "PT12", "SH3", "C2,1", "C2,2", "OT13", "C2,3", "C-3,0", "C-3,1", "C-3,2", "PT13",
+    "PT03", "SH4", "C-3,3", "C3,0", "C3,1", "W3", "C3,2", "C3,3", "W4",
 )
 OFFSET = {}
 TOTAL = 0
@@ -42,7 +42,7 @@
     slots, count, feat, tiles_hbm, weight_hbm, cot_hbm,
     layer_out, weight_grad, feature_grad,
     tiles, xpan, pacc, ks, kr, sxs, sx, rx, zs, rz, qs, rq, xfs, xfr, zf,
-    hp, lt, acc, w1s, w1r, w2s, w2r, w3r, w4r, w5r, gs, gr, weight, cot, inv_v, inv,
+    hp, acc, w1s, w1r, w2s, w2r, w3r, w4r, w5r, gs, gr, weight, cot, inv_v, inv,
     ssem, rsem, tsem,
 ):
     r = lax.axis_index("row")
@@ -240,7 +240,7 @@
     sig = jax.nn.sigmoid(preact)
     layer_out[...] = (preact * sig).astype(BF16)
     act = (cot[...].astype(F32) * sig * (1.0 + preact * (1.0 - sig))).astype(BF16)
-    hp[z, k, xl] = jnp.dot(act, weight[...].T, preferred_element_type=F32).astype(BF16)
+    hp[z, k, xl] = jnp.dot(weight[...], act.T, preferred_element_type=F32).astype(BF16)
 
     head_rows, tail_rows = pl.ds(0, B), pl.ds(B, N - B)
     mine = hp.at[z, k, xl]
@@ -294,11 +294,22 @@
 
     def have(d):
         arrive(hp.at[place(d), ok], "pair", number(d))
-        lt[...] = jnp.concatenate([hp[place(d), q // 2, q % 2] for q in range(4)], axis=0).T
-
-    def add_product(d, n):
-        rows = [pair(2 * (((q // 2) % 2) * 16 + place(d) * 2 + q // 4) + q % 2, n) for q in range(8)]
-        acc[n] += jnp.dot(lt[...], jnp.concatenate(rows, axis=0), preferred_element_type=F32)
+
+    def add_product(d, n, own=None):
+        blocks = [(k, xl), (k, ox), (ok, xl), (ok, ox)] if abs(d) < 2 else [(q // 2, q % 2) for q in range(4)]
+        blocks = blocks if own is None else blocks[:1] if own else blocks[1:]
+        left = jnp.concatenate([hp[place(d), u, v] for u, v in blocks], axis=1)
+        rows = [pair(2 * (v * 16 + place(d) * 2 + u) + q, n) for u, v in blocks for q in range(2)]
+        total = jnp.dot(left, jnp.concatenate(rows, axis=0), preferred_element_type=F32)
+        if own and d == 0:
+            acc[n] = total
+        else:
+            acc[n] += total
+
+    def own_block(d):
+        @pl.loop(0, 8)
+        def _(n):
+            add_product(d, n, True)
 
     def backward(d, part):
         if part == 0:
@@ -306,7 +317,7 @@
 
         @pl.loop(2 * part, 2 * part + 2)
         def _(n):
-            add_product(d, n)
+            add_product(d, n, False if abs(d) < 2 else None)
 
     def x_tail():
         rows = hp.at[z, k, ox, tail_rows]
@@ -319,7 +330,6 @@
             w1s[...] = jnp.dot(hidden.T, act, preferred_element_type=F32).reshape(8, 32, N)
             for i in range(1, 8):
                 send(w1s.at[row_of(i)], w1r.at[r], "w1", i, at_row(i))
-            acc[...] = jnp.zeros_like(acc)
         elif step == 2:
             for i in range(1, 8):
                 arrive(w1r.at[row_from(i)], "w1", i)
@@ -363,6 +373,8 @@
             part_step(int(op[2]), int(op[3]))
         elif op[:2] == "SH":
             share(int(op[2:]))
+        elif op[0] == "B":
+            own_block(int(op[1:]))
         elif op[0] == "C":
             d, part = op[1:].split(",")
             backward(int(d), int(part))
@@ -443,7 +455,6 @@
             buf(N - A, N),
             buf(N - A, N, dtype=F32),
             buf(8, 2, 2, N, N),
-            buf(N, 4 * N),
             buf(8, N, N, dtype=F32),
             buf(8, 32, N, dtype=F32),
             buf(8, 32, N, dtype=F32),

time: 101 us -> 102 us (level)
  no operation moved by 1% of the time
where the time goes in v4:
time: 102 us; the launch traced here: 101 us
  Pallas kernels  100 us (98%)
  between operations  1.29 us (1%)
    pallas_call x1, Pallas kernels, body(): pl.pallas_call(kernel, out_shape=shapes, in_specs=[smem, smem, hbm, hbm,...  98.3 us

profile of v4, /device:TPU:1, one launch (start us, length us, event | category | flops | bytes accessed | tf_op | source)
XLA Modules:
  0.0 101.4 jit_solution(1507520654889852366)
XLA Ops:
  1.3 98.3 %shard_map.85 = (bf16[256,256]{1,0:T(8,128)(2,1)}, f32[256,256]{1,0:T(8,128)}, bf16[256,256]{1,0:T(8,128)(2,1)}) custom-call(s32[1,192]{1,0:T(1,128)} %slots.1, s32[1,1]{1,0:T(1,128)S(6)} %copy.9.count, bf16[256,256]{1,0:T(8,128)(2,1)} %feat.1, bf16[192,128,128]{2,1,0:T(8,128)(2,1)} %bitcast.1, bf16[256,256]{1,0:T(8,128)(2,1)} %weight_hbm.1, ...), custom_call_target="tpu_custom_call" | custom-call | tf_op jit(solution)/shard_map/pallas_call | solution.py:436
  99.6 1.8 %shard_map.86 = (bf16[256,256]{1,0:T(8,128)(2,1)}, f32[256,256]{1,0:T(8,128)}, bf16[256,256]{1,0:T(8,128)(2,1)}) custom-call(bf16[256,256]{1,0:T(8,128)(2,1)} %get-tuple-element.6.a, f32[256,256]{1,0:T(8,128)} %get-tuple-element.7.b, bf16[256,256]{1,0:T(8,128)(2,1)} %get-tuple-element.8.c), custom_call_target="tpu_custom_call" | custom-call | tf_op jit(solution)/shard_map/pallas_call | solution.py:480

commit v5 on v4

--- a/solution.py
+++ b/solution.py
@@ -26,10 +26,10 @@
 )
 GATHER = (
     "B0", "OH00", "OH10", "V", "W1", "OT10", "OT00", "SH0", "B1", "B-1", "C0,0", "C0,1", "OH01", "OH11", "C0,2",
-    "C0,3", "PT00", "SH-1", "PT10", "SH1", "OT01", "OT11", "C-1,0", "C-1,1", "C-1,2", "C-1,3", "OH12", "OH02", "C1,0",
-    "C1,1", "W2", "PT01", "PT11", "SH-2", "C1,2", "C1,3", "SH2", "OT02", "OT12", "C-2,0", "C-2,1", "OH03", "C-2,2",
-    "C-2,3", "C2,0", "PT02", "SH-3", "PT12", "SH3", "C2,1", "C2,2", "OT13", "C2,3", "C-3,0", "C-3,1", "C-3,2", "PT13",
-    "PT03", "SH4", "C-3,3", "C3,0", "C3,1", "W3", "C3,2", "C3,3", "W4",
+    "C0,3", "PT00", "SH-1", "PT10", "SH1", "OT01", "OT11", "C-1,0", "C-1,1", "W2", "C-1,2", "C-1,3", "OH12", "OH02",
+    "C1,0", "C1,1", "PT01", "PT11", "SH-2", "C1,2", "C1,3", "SH2", "OT02", "OT12", "C-2,0", "C-2,1", "OH03", "C-2,2",
+    "C-2,3", "C2,0", "PT02", "SH-3", "PT12", "SH3", "C2,1", "C2,2", "OT13", "C2,3", "W3", "C-3,0", "C-3,1", "C-3,2",
+    "PT13", "PT03", "SH4", "C-3,3", "W4", "C3,0", "C3,1", "C3,2", "C3,3",
 )
 OFFSET = {}
 TOTAL = 0
@@ -120,28 +120,39 @@
     place_table.wait()
     local[1].wait()
 
-    def pair(row, p):
-        n, at = row // 8, (row % 8) * 16 + 2 * p
+    two = jnp.int32(2)
+
+    def spot(zt):
+        return zt, lax.div(zt, two), lax.rem(zt, two) * 64
+
+    def pair(n, at):
         return jnp.concatenate([tiles[inv[n, at]], tiles[inv[n, at + 1]]], axis=1)
 
-    def product(zt, kt, blocks):
+    def product(where, kt, blocks):
+        _, half, begin = where
+        begin = begin + kt * 32
         total = None
         for p in blocks:
-            rows = [pair(2 * ((q // 2) * 16 + zt * 2 + kt) + q % 2, p) for q in range(4)]
+            at = begin + 2 * p
+            rows = [pair(half + (q // 2) * 4, at + (q % 2) * 16) for q in range(4)]
             part = jnp.dot(jnp.concatenate(rows, axis=0), xpan[p], preferred_element_type=F32)
             total = part if total is None else total + part
         return total
 
     @pl.loop(0, 16)
     def _(j):
-        pacc[j // 2, j % 2] = product(j // 2, j % 2, [r])
+        zt, kt = lax.div(j, two), lax.rem(j, two)
+        pacc[zt, kt] = product(spot(zt), kt, [r])
 
     for i in (1, 3, 4):
         arrive(xpan.at[row_from(i)], "feat", i)
+    early = [row_from(i) for i in (1, 3, 4)]
+    late = [row_from(i) for i in (2, 5, 7, 6)]
 
     @pl.loop(0, 16)
     def _(j):
-        pacc[j // 2, j % 2] += product(j // 2, j % 2, [row_from(i) for i in (1, 3, 4)])
+        zt, kt = lax.div(j, two), lax.rem(j, two)
+        pacc[zt, kt] += product(spot(zt), kt, early)
 
     for i in (2, 5, 7, 6):
         arrive(xpan.at[row_from(i)], "feat", i)
@@ -152,7 +163,7 @@
     def forward(g, h):
         zt = (z + DIST[g] + 8) % 8
         kt = k if h else ok
-        pacc[zt, kt] += product(zt, kt, [row_from(i) for i in (2, 5, 7, 6)])
+        pacc[zt, kt] += product(spot(zt), kt, late)
         if h == 0:
             for q in range(2):
                 ks[g, q] = pacc[zt, kt, pl.ds(q * N, N)].astype(BF16)
@@ -295,29 +306,36 @@
     def have(d):
         arrive(hp.at[place(d), ok], "pair", number(d))
 
-    def add_product(d, n, own=None):
-        blocks = [(k, xl), (k, ox), (ok, xl), (ok, ox)] if abs(d) < 2 else [(q // 2, q % 2) for q in range(4)]
-        blocks = blocks if own is None else blocks[:1] if own else blocks[1:]
-        left = jnp.concatenate([hp[place(d), u, v] for u, v in blocks], axis=1)
-        rows = [pair(2 * (v * 16 + place(d) * 2 + u) + q, n) for u, v in blocks for q in range(2)]
+    def add_product(where, blocks, n, first=False):
+        zt, half, begin = where
+        left = jnp.concatenate([hp[zt, u, v] for u, v in blocks], axis=1)
+        rows = [
+            pair(half + v * 4, begin + u * 32 + 2 * n + q * 16) for u, v in blocks for q in range(2)
+        ]
         total = jnp.dot(left, jnp.concatenate(rows, axis=0), preferred_element_type=F32)
-        if own and d == 0:
+        if first:
             acc[n] = total
         else:
             acc[n] += total
 
+    every = [(0, 0), (0, 1), (1, 0), (1, 1)]
+    others = [(k, ox), (ok, xl), (ok, ox)]
+
     def own_block(d):
+        where = spot(place(d))
+
         @pl.loop(0, 8)
         def _(n):
-            add_product(d, n, True)
+            add_product(where, [(k, xl)], n, d == 0)
 
     def backward(d, part):
         if part == 0:
             have(d)
+        where = spot(place(d))
 
         @pl.loop(2 * part, 2 * part + 2)
         def _(n):
-            add_product(d, n, False if abs(d) < 2 else None)
+            add_product(where, others if abs(d) < 2 else every, n)
 
     def x_tail():
         rows = hp.at[z, k, ox, tail_rows]
@@ -384,12 +402,13 @@
             x_tail()
 
     have(4)
+    farthest = spot(place(4))
 
     @pl.loop(0, 8)
     def _(j):
         i = (j + 1) % 8
         n = row_of(i)
-        add_product(4, n)
+        add_product(farthest, every, n)
 
         @pl.when(i != 0)
         def _():

time: 102 us -> 101 us (level)
  no operation moved by 1% of the time
where the time goes in v5:
time: 101 us
  Pallas kernels  99.4 us (98%)
  between operations  1.29 us (1%)
    pallas_call x1, Pallas kernels, body(): pl.pallas_call(kernel, out_shape=shapes, in_specs=[smem, smem, hbm, hbm,...  97.6 us

profile of v5, /device:TPU:1, one launch (start us, length us, event | category | flops | bytes accessed | tf_op | source)
XLA Modules:
  0.0 100.7 jit_solution(9547752873939791625)
XLA Ops:
  1.3 97.6 %shard_map.85 = (bf16[256,256]{1,0:T(8,128)(2,1)}, f32[256,256]{1,0:T(8,128)}, bf16[256,256]{1,0:T(8,128)(2,1)}) custom-call(s32[1,192]{1,0:T(1,128)} %slots.1, s32[1,1]{1,0:T(1,128)S(6)} %copy.9.count, bf16[256,256]{1,0:T(8,128)(2,1)} %feat.1, bf16[192,128,128]{2,1,0:T(8,128)(2,1)} %bitcast.1, bf16[256,256]{1,0:T(8,128)(2,1)} %weight_hbm.1, ...), custom_call_target="tpu_custom_call" | custom-call | tf_op jit(solution)/shard_map/pallas_call | solution.py:455
  98.8 1.8 %shard_map.86 = (bf16[256,256]{1,0:T(8,128)(2,1)}, f32[256,256]{1,0:T(8,128)}, bf16[256,256]{1,0:T(8,128)(2,1)}) custom-call(bf16[256,256]{1,0:T(8,128)(2,1)} %get-tuple-element.6.a, f32[256,256]{1,0:T(8,128)} %get-tuple-element.7.b, bf16[256,256]{1,0:T(8,128)(2,1)} %get-tuple-element.8.c), custom_call_target="tpu_custom_call" | custom-call | tf_op jit(solution)/shard_map/pallas_call | solution.py:499

commit v6 on v5

--- a/solution.py
+++ b/solution.py
@@ -306,17 +306,20 @@
     def have(d):
         arrive(hp.at[place(d), ok], "pair", number(d))
 
-    def add_product(where, blocks, n, first=False):
+    def add_products(where, blocks, places, first=False):
         zt, half, begin = where
         left = jnp.concatenate([hp[zt, u, v] for u, v in blocks], axis=1)
-        rows = [
-            pair(half + v * 4, begin + u * 32 + 2 * n + q * 16) for u, v in blocks for q in range(2)
-        ]
-        total = jnp.dot(left, jnp.concatenate(rows, axis=0), preferred_element_type=F32)
-        if first:
-            acc[n] = total
-        else:
-            acc[n] += total
+        totals = []
+        for n in places:
+            rows = [
+                pair(half + v * 4, begin + u * 32 + 2 * n + q * 16) for u, v in blocks for q in range(2)
+            ]
+            totals.append(jnp.dot(left, jnp.concatenate(rows, axis=0), preferred_element_type=F32))
+        for n, total in zip(places, totals):
+            if first:
+                acc[n] = total
+            else:
+                acc[n] += total
 
     every = [(0, 0), (0, 1), (1, 0), (1, 1)]
     others = [(k, ox), (ok, xl), (ok, ox)]
@@ -324,18 +327,14 @@
     def own_block(d):
         where = spot(place(d))
 
-        @pl.loop(0, 8)
-        def _(n):
-            add_product(where, [(k, xl)], n, d == 0)
+        for n in (0, 4):
+            add_products(where, [(k, xl)], [n, n + 1, n + 2, n + 3], d == 0)
 
     def backward(d, part):
         if part == 0:
             have(d)
         where = spot(place(d))
-
-        @pl.loop(2 * part, 2 * part + 2)
-        def _(n):
-            add_product(where, others if abs(d) < 2 else every, n)
+        add_products(where, others if abs(d) < 2 else every, [2 * part, 2 * part + 1])
 
     def x_tail():
         rows = hp.at[z, k, ox, tail_rows]
@@ -404,16 +403,12 @@
     have(4)
     farthest = spot(place(4))
 
-    @pl.loop(0, 8)
-    def _(j):
-        i = (j + 1) % 8
-        n = row_of(i)
-        add_product(farthest, every, n)
-
-        @pl.when(i != 0)
-        def _():
-            gs[n] = acc[n].astype(BF16)
-            desc(gs.at[n], gr.at[r], "grad", i, at_row(i)).start()
+    for group in ((6, 5), (7, 2), (4, 1), (3, 0)):
+        add_products(farthest, every, [row_of(i) for i in group])
+        for i in group:
+            if i:
+                gs[row_of(i)] = acc[row_of(i)].astype(BF16)
+                send(gs.at[row_of(i)], gr.at[r], "grad", i, at_row(i))
 
     gradient_step(5)
     s = acc[r]
@@ -429,8 +424,6 @@
             weight_grad[first:first + 8, (i % 2) * 128:(i % 2) * 128 + 128] = w5r[i, j] * (65536.0 ** -0.5)
     for d in sent:
         d.wait_send()
-    for i in range(1, 8):
-        desc(gs.at[row_of(i)], gr.at[r], "grad", i, at_row(i)).wait_send()
 
 
 def hand_over(a, b, c, a_out, b_out, c_out):

time: 101 us -> 95.5 us (0.946)
  the two profiles are of different devices: /device:TPU:1 before, /device:TPU:16 now
where the time goes in v6:
time: 95.5 us; the launch traced here: 95.4 us
  Pallas kernels  94.1 us (99%)
  between operations  1.29 us (1%)
    pallas_call x1, Pallas kernels, body(): pl.pallas_call(kernel, out_shape=shapes, in_specs=[smem, smem, hbm, hbm,...  92.3 us

profile of v6, /device:TPU:16, one launch (start us, length us, event | category | flops | bytes accessed | tf_op | source)
XLA Modules:
  0.0 95.4 jit_solution(6314286235506028793)
XLA Ops:
  1.3 92.3 %shard_map.85 = (bf16[256,256]{1,0:T(8,128)(2,1)}, f32[256,256]{1,0:T(8,128)}, bf16[256,256]{1,0:T(8,128)(2,1)}) custom-call(s32[1,192]{1,0:T(1,128)} %slots.1, s32[1,1]{1,0:T(1,128)S(6)} %copy.9.count, bf16[256,256]{1,0:T(8,128)(2,1)} %feat.1, bf16[192,128,128]{2,1,0:T(8,128)(2,1)} %bitcast.1, bf16[256,256]{1,0:T(8,128)(2,1)} %weight_hbm.1, ...), custom_call_target="tpu_custom_call" | custom-call | tf_op jit(solution)/shard_map/pallas_call | solution.py:448
  93.5 1.8 %shard_map.86 = (bf16[256,256]{1,0:T(8,128)(2,1)}, f32[256,256]{1,0:T(8,128)}, bf16[256,256]{1,0:T(8,128)(2,1)}) custom-call(bf16[256,256]{1,0:T(8,128)(2,1)} %get-tuple-element.6.a, f32[256,256]{1,0:T(8,128)} %get-tuple-element.7.b, bf16[256,256]{1,0:T(8,128)(2,1)} %get-tuple-element.8.c), custom_call_target="tpu_custom_call" | custom-call | tf_op jit(solution)/shard_map/pallas_call | solution.py:492

commit v7 on v6

--- a/solution.py
+++ b/solution.py
@@ -15,7 +15,7 @@
 B = 128
 DIST = (4, 3, -3, 2, -2, 1, -1, 0)
 SEMS = dict(
-    feat=8, core=8, xrow=8, ringz=16, ringx=8, xfin=1,
+    feat=12, core=8, xrow=8, ringz=16, ringx=8, xfin=1,
     head=8, tail=8, part=8, xv=1, xu=8, pair=8,
     w1=8, w2=8, w3=4, w4=8, w5=8, grad=8,
 )
@@ -115,8 +115,17 @@
     local[0].wait()
     pl.semaphore_wait(barrier, 17)
 
-    for i in (4, 1, 3, 2, 5, 7, 6):
-        send(xpan.at[r], xpan.at[r], "feat", i, at_row(i))
+    def feature(i, lower=None):
+        block = xpan.at[row_from(i)]
+        return block if lower is None else block.at[pl.ds(128 * lower, 128)]
+
+    def pass_on(i, lower, name, to):
+        send(feature(i, lower), feature(i, lower), "feat", name, at_row(to))
+
+    pass_on(0, 1, 0, 4)
+    for i in (1, 3, 2):
+        pass_on(0, None, i, i)
+    pass_on(0, 0, 4, 4)
     place_table.wait()
     local[1].wait()
 
@@ -144,18 +153,29 @@
         zt, kt = lax.div(j, two), lax.rem(j, two)
         pacc[zt, kt] = product(spot(zt), kt, [r])
 
-    for i in (1, 3, 4):
-        arrive(xpan.at[row_from(i)], "feat", i)
-    early = [row_from(i) for i in (1, 3, 4)]
-    late = [row_from(i) for i in (2, 5, 7, 6)]
-
-    @pl.loop(0, 16)
-    def _(j):
-        zt, kt = lax.div(j, two), lax.rem(j, two)
-        pacc[zt, kt] += product(spot(zt), kt, early)
-
-    for i in (2, 5, 7, 6):
-        arrive(xpan.at[row_from(i)], "feat", i)
+    arrive(feature(4, 1), "feat", 0)
+    for i in (1, 3, 2):
+        pass_on(4, 1, 4 + i, i)
+    for i in (1, 3):
+        arrive(feature(i), "feat", i)
+        pass_on(i, 0, 8 + i, 4)
+    late = [row_from(i) for i in (4, 5, 7, 6)]
+
+    def add_early(first, last, places):
+        @pl.loop(first, last)
+        def _(j):
+            zt, kt = lax.div(j, two), lax.rem(j, two)
+            pacc[zt, kt] += product(spot(zt), kt, [row_from(i) for i in places])
+
+    add_early(0, 8, (1, 3))
+    arrive(feature(2), "feat", 2)
+    pass_on(2, 0, 10, 4)
+    add_early(8, 16, (1, 3))
+    add_early(0, 16, (2,))
+    arrive(feature(4, 0), "feat", 4)
+    for i in (1, 3, 2):
+        arrive(feature(4 + i, 1), "feat", 4 + i)
+        arrive(feature(4 + i, 0), "feat", 8 + i)
 
     def side(q):
         return xl if q else ox
@@ -412,10 +432,10 @@
 
     gradient_step(5)
     s = acc[r]
-    for i in range(1, 8):
+    for i in (6, 5, 7, 2, 4, 1, 3):
         arrive(gr.at[row_from(i)], "grad", i)
         s = s + gr[row_from(i)].astype(F32)
-    feature_grad[...] = s.T.astype(BF16)
+    feature_grad[...] = s.astype(BF16).T
     for i in range(1, 8):
         arrive(w5r.at[place(-i)], "w5", i)
     for i in range(8):

time: 95.5 us -> 93.9 us (0.983)
  the two profiles are of different devices: /device:TPU:16 before, /device:TPU:1 now
where the time goes in v7:
time: 93.9 us; the launch traced here: 93.7 us
  Pallas kernels  92.4 us (98%)
  between operations  1.29 us (1%)
    pallas_call x1, Pallas kernels, body(): pl.pallas_call(kernel, out_shape=shapes, in_specs=[smem, smem, hbm, hbm,...  90.6 us

profile of v7, /device:TPU:1, one launch (start us, length us, event | category | flops | bytes accessed | tf_op | source)
XLA Modules:
  0.0 93.7 jit_solution(13620127194659603127)
XLA Ops:
  1.3 90.6 %shard_map.85 = (bf16[256,256]{1,0:T(8,128)(2,1)}, f32[256,256]{1,0:T(8,128)}, bf16[256,256]{1,0:T(8,128)(2,1)}) custom-call(s32[1,192]{1,0:T(1,128)} %slots.1, s32[1,1]{1,0:T(1,128)S(6)} %copy.9.count, bf16[256,256]{1,0:T(8,128)(2,1)} %feat.1, bf16[192,128,128]{2,1,0:T(8,128)(2,1)} %bitcast.1, bf16[256,256]{1,0:T(8,128)(2,1)} %weight_hbm.1, ...), custom_call_target="tpu_custom_call" | custom-call | tf_op jit(solution)/shard_map/pallas_call | solution.py:468
  91.9 1.8 %shard_map.86 = (bf16[256,256]{1,0:T(8,128)(2,1)}, f32[256,256]{1,0:T(8,128)}, bf16[256,256]{1,0:T(8,128)(2,1)}) custom-call(bf16[256,256]{1,0:T(8,128)(2,1)} %get-tuple-element.6.a, f32[256,256]{1,0:T(8,128)} %get-tuple-element.7.b, bf16[256,256]{1,0:T(8,128)(2,1)} %get-tuple-element.8.c), custom_call_target="tpu_custom_call" | custom-call | tf_op jit(solution)/shard_map/pallas_call | solution.py:512

commit v8 on v7

--- a/solution.py
+++ b/solution.py
@@ -29,7 +29,7 @@
     "C0,3", "PT00", "SH-1", "PT10", "SH1", "OT01", "OT11", "C-1,0", "C-1,1", "W2", "C-1,2", "C-1,3", "OH12", "OH02",
     "C1,0", "C1,1", "PT01", "PT11", "SH-2", "C1,2", "C1,3", "SH2", "OT02", "OT12", "C-2,0", "C-2,1", "OH03", "C-2,2",
     "C-2,3", "C2,0", "PT02", "SH-3", "PT12", "SH3", "C2,1", "C2,2", "OT13", "C2,3", "W3", "C-3,0", "C-3,1", "C-3,2",
-    "PT13", "PT03", "SH4", "C-3,3", "W4", "C3,0", "C3,1", "C3,2", "C3,3",
+    "PT13", "PT03", "SH4", "C-3,3", "W4",
 )
 OFFSET = {}
 TOTAL = 0
@@ -420,11 +420,13 @@
         else:
             x_tail()
 
+    have(3)
     have(4)
-    farthest = spot(place(4))
+    far, farthest = spot(place(3)), spot(place(4))
 
     for group in ((6, 5), (7, 2), (4, 1), (3, 0)):
-        add_products(farthest, every, [row_of(i) for i in group])
+        for where in (far, farthest):
+            add_products(where, every, [row_of(i) for i in group])
         for i in group:
             if i:
                 gs[row_of(i)] = acc[row_of(i)].astype(BF16)

time: 93.9 us -> 94 us (level)
  no operation moved by 1% of the time
where the time goes in v8:
time: 94 us; the launch traced here: 93.8 us
  Pallas kernels  92.6 us (99%)
  between operations  1.29 us (1%)
    pallas_call x1, Pallas kernels, body(): pl.pallas_call(kernel, out_shape=shapes, in_specs=[smem, smem, hbm, hbm,...  90.7 us

profile of v8, /device:TPU:1, one launch (start us, length us, event | category | flops | bytes accessed | tf_op | source)
XLA Modules:
  0.0 93.8 jit_solution(101496659270136525)
XLA Ops:
  1.3 90.7 %shard_map.85 = (bf16[256,256]{1,0:T(8,128)(2,1)}, f32[256,256]{1,0:T(8,128)}, bf16[256,256]{1,0:T(8,128)(2,1)}) custom-call(s32[1,192]{1,0:T(1,128)} %slots.1, s32[1,1]{1,0:T(1,128)S(6)} %copy.9.count, bf16[256,256]{1,0:T(8,128)(2,1)} %feat.1, bf16[192,128,128]{2,1,0:T(8,128)(2,1)} %bitcast.1, bf16[256,256]{1,0:T(8,128)(2,1)} %weight_hbm.1, ...), custom_call_target="tpu_custom_call" | custom-call | tf_op jit(solution)/shard_map/pallas_call | solution.py:470
  92.0 1.8 %shard_map.86 = (bf16[256,256]{1,0:T(8,128)(2,1)}, f32[256,256]{1,0:T(8,128)}, bf16[256,256]{1,0:T(8,128)(2,1)}) custom-call(bf16[256,256]{1,0:T(8,128)(2,1)} %get-tuple-element.6.a, f32[256,256]{1,0:T(8,128)} %get-tuple-element.7.b, bf16[256,256]{1,0:T(8,128)(2,1)} %get-tuple-element.8.c), custom_call_target="tpu_custom_call" | custom-call | tf_op jit(solution)/shard_map/pallas_call | solution.py:514

commit v9 on v8

--- a/solution.py
+++ b/solution.py
@@ -28,8 +28,8 @@
     "B0", "OH00", "OH10", "V", "W1", "OT10", "OT00", "SH0", "B1", "B-1", "C0,0", "C0,1", "OH01", "OH11", "C0,2",
     "C0,3", "PT00", "SH-1", "PT10", "SH1", "OT01", "OT11", "C-1,0", "C-1,1", "W2", "C-1,2", "C-1,3", "OH12", "OH02",
     "C1,0", "C1,1", "PT01", "PT11", "SH-2", "C1,2", "C1,3", "SH2", "OT02", "OT12", "C-2,0", "C-2,1", "OH03", "C-2,2",
-    "C-2,3", "C2,0", "PT02", "SH-3", "PT12", "SH3", "C2,1", "C2,2", "OT13", "C2,3", "W3", "C-3,0", "C-3,1", "C-3,2",
-    "PT13", "PT03", "SH4", "C-3,3", "W4",
+    "C-2,3", "C2,0", "PT02", "SH-3", "PT12", "SH3", "C2,1", "W3", "C2,2", "OT13", "C2,3", "C-3,0", "C-3,1", "W4", "C-3,2",
+    "PT13", "PT03", "SH4", "C-3,3",
 )
 OFFSET = {}
 TOTAL = 0

time: 94 us -> 94.4 us (level)
  no operation moved by 1% of the time
where the time goes in v9:
time: 94.4 us; the launch traced here: 94.3 us
  Pallas kernels  93 us (99%)
  between operations  1.29 us (1%)
    pallas_call x1, Pallas kernels, body(): pl.pallas_call(kernel, out_shape=shapes, in_specs=[smem, smem, hbm, hbm,...  91.2 us

profile of v9, /device:TPU:1, one launch (start us, length us, event | category | flops | bytes accessed | tf_op | source)
XLA Modules:
  0.0 94.3 jit_solution(9374149541848407398)
XLA Ops:
  1.3 91.2 %shard_map.85 = (bf16[256,256]{1,0:T(8,128)(2,1)}, f32[256,256]{1,0:T(8,128)}, bf16[256,256]{1,0:T(8,128)(2,1)}) custom-call(s32[1,192]{1,0:T(1,128)} %slots.1, s32[1,1]{1,0:T(1,128)S(6)} %copy.9.count, bf16[256,256]{1,0:T(8,128)(2,1)} %feat.1, bf16[192,128,128]{2,1,0:T(8,128)(2,1)} %bitcast.1, bf16[256,256]{1,0:T(8,128)(2,1)} %weight_hbm.1, ...), custom_call_target="tpu_custom_call" | custom-call | tf_op jit(solution)/shard_map/pallas_call | solution.py:470
  92.5 1.8 %shard_map.86 = (bf16[256,256]{1,0:T(8,128)(2,1)}, f32[256,256]{1,0:T(8,128)}, bf16[256,256]{1,0:T(8,128)(2,1)}) custom-call(bf16[256,256]{1,0:T(8,128)(2,1)} %get-tuple-element.6.a, f32[256,256]{1,0:T(8,128)} %get-tuple-element.7.b, bf16[256,256]{1,0:T(8,128)(2,1)} %get-tuple-element.8.c), custom_call_target="tpu_custom_call" | custom-call | tf_op jit(solution)/shard_map/pallas_call | solution.py:514
